TPU v7x, 256 devices: a whole 4x4x8 slice. The times are simulated.
256 devices in a mesh: dom: 64 (over z, x, core), rep: 4 (over y).
Axes of the slice: x: 4, y: 4, z: 8, core: 2. Of those that a mesh axis runs over, the one named last changes fastest.
Arguments:
- history: bfloat16 [131072, 256], P('dom'), may hold values from -6 to 6
- batch_ids: int32 [262144], P(('dom', 'rep')), may hold values from 0 to 2047
- halo_ids: int32 [256, 64, 32], P(('dom', 'rep')), may hold values from 0 to 2047
- halo_counts: int32 [256, 64], P(('dom', 'rep')), may hold values from 1 to 32, as said below
- adj_local: bfloat16 [262144, 1024], P(('dom', 'rep')), may hold values from -0.109375 to 0.109375
- adj_halo: bfloat16 [262144, 2048], P(('dom', 'rep')), may hold values from -0.109375 to 0.109375
- weight: bfloat16 [256, 256], replicated, may hold values from -0.375 to 0.375
- cotangent: bfloat16 [262144, 256], P(('dom', 'rep')), may hold values from -6 to 6
Outputs:
- layer_out: bfloat16 [262144, 256], P(('dom', 'rep'))
- grad_weight: float32 [256, 256], replicated
- history_grad: float32 [131072, 256], P('dom')
Inputs may be any that keep to these rules, and one draw needn't show every extreme that they name: `halo_counts`: every device takes from every owner between 1 and 32 rows; for some owners every device takes exactly 32. `halo_ids`: rows of the owner's history; slots at or past the used count are unused. `batch_ids`: rows of the device's own partition's history; may repeat.
All inputs are finite; a program needn't handle non-finite values.
Results may differ from a plain program's by a relative error of at most 0.0065.
Values may be sent and summed in bfloat16 or wider, within the bound.
No kernel may reach another device: no remote copies, remote signals or barrier semaphores. Data moves between devices by JAX's collectives and lax.ppermute only.
A program may use at most 64 MiB of HBM per device.

v0:
```python
import jax
import jax.numpy as jnp
from jax import lax
from jax.experimental import pallas as pl
from jax.experimental.pallas import tpu as pltpu
from jax.sharding import PartitionSpec as P

BF16, F32, I32 = jnp.bfloat16, jnp.float32, jnp.int32
VMEM = pl.BlockSpec(memory_space=pltpu.VMEM)
SMEM = pl.BlockSpec(memory_space=pltpu.SMEM)
ANY = pl.BlockSpec(memory_space=pl.ANY)


def vmem_call(kernel, out_shape, in_specs, flops=0, moved=0, scratch=()):
    return pl.pallas_call(
        kernel,
        out_shape=out_shape,
        in_specs=in_specs,
        out_specs=jax.tree.map(lambda _: VMEM, out_shape),
        scratch_shapes=list(scratch),
        compiler_params=pltpu.CompilerParams(vmem_limit_bytes=16 * 1024 * 1024),
        cost_estimate=pl.CostEstimate(flops=flops, bytes_accessed=moved, transcendentals=0),
    )


def spread_column(columns, i):
    return jnp.broadcast_to(columns[:, i : i + 1], (columns.shape[0], 128))


def gather_kernel(ids_ref, table_ref, out_ref):
    nodes, (groups, size) = table_ref.shape[0], ids_ref.shape
    columns = ids_ref[...].T
    lane = lax.broadcasted_iota(I32, (256, 128), 1)
    for step in range(out_ref.shape[0] // 256):
        many = 256 // size
        column = jnp.concatenate([spread_column(columns, step * many + i) for i in range(many)], 0)
        picks = jnp.concatenate(
            [jnp.where(column == lane + base, 1.0, 0.0).astype(BF16) for base in range(0, nodes, 128)], 1
        )
        rows = jnp.dot(picks, table_ref[...], preferred_element_type=F32)
        out_ref[256 * step : 256 * step + 256, :] = rows.astype(BF16)


def gather_rows(table, ids):
    count, (nodes, width) = ids.size, table.shape
    return vmem_call(
        gather_kernel,
        jax.ShapeDtypeStruct((count, width), BF16),
        [VMEM, VMEM],
        flops=2 * count * nodes * width,
        moved=4 * count * width,
    )(ids, table)


def pack_pair(first, second, part):
    block = slice(128 * (part // 2), 128 * (part // 2) + 128)
    left = lax.broadcasted_iota(I32, (first.shape[0], 128), 1) < 64
    if part % 2 == 0:
        return jnp.where(left, first[:, block], pltpu.roll(second[:, block], 64, 1))
    return jnp.where(left, pltpu.roll(first[:, block], 64, 1), second[:, block])


def middle_kernel(
    counts_ref, rep_ref, rows_hbm, adj_hbm, local_hbm, weight_hbm, cotangent_hbm, adj_local_hbm,
    out_hbm, part_hbm, messages_hbm, *refs,
):
    local_hbms, refs = refs[:4], refs[4:]
    rows_ref, adj_ref, local_ref, weight_ref, cotangent_ref, adj_local_ref, *refs = refs
    out_ref, part_ref, packed_ref, parts_ref, live_ref, agg_ref, grad_pre_ref, grads_ref, sums_ref, load_sems, store_sems = refs
    slots, owners = 32, 64
    half = sums_ref.shape[0] // 2
    chunks = [slice(base, base + 256) for base in range(0, 2 * half, 256)]

    loads, stores = [], []

    def load(source, target):
        loads.append(pltpu.make_async_copy(source, target, load_sems.at[len(loads)]))
        loads[-1].start()
        return loads[-1]

    def store(source, target):
        stores.append(pltpu.make_async_copy(source, target, store_sems.at[len(stores)]))
        stores[-1].start()

    rows_in = load(rows_hbm, rows_ref)
    adj_in = [load(adj_hbm.at[chunks[0]], adj_ref.at[chunks[0]])]
    weight_in, local_in = load(weight_hbm, weight_ref), load(local_hbm, local_ref)
    cotangent_in = load(cotangent_hbm, cotangent_ref)
    adj_in += [load(adj_hbm.at[at], adj_ref.at[at]) for at in chunks[1:]]
    adj_local_in = load(adj_local_hbm, adj_local_ref)

    slot = lax.broadcasted_iota(I32, (slots, 256), 0)
    rows_in.wait()
    for owner in range(owners):
        at = slice(slots * owner, slots * owner + slots)
        live = jnp.where(slot < counts_ref[0, owner], rows_ref[at, :].astype(F32), 0.0)
        live_ref[at, :] = live.astype(BF16)
    for i, at in enumerate(chunks):
        adj_in[i].wait()
        if i == 0:
            weight_in.wait()
            local_in.wait()
            cotangent_in.wait()
        summed = local_ref[at, :] + jnp.dot(adj_ref[at, :], live_ref[...], preferred_element_type=F32)
        agg = summed.astype(BF16)
        agg_ref[at, :] = agg
        pre_act = jnp.dot(agg, weight_ref[...], preferred_element_type=F32)
        gate = jax.nn.sigmoid(pre_act)
        out_ref[at, :] = (pre_act * gate).astype(BF16)
        grad_pre = (cotangent_ref[at, :].astype(F32) * gate * (1.0 + pre_act * (1.0 - gate))).astype(BF16)
        grad_pre_ref[at, :] = grad_pre
        grads_ref[at, :] = lax.dot_general(
            grad_pre, weight_ref[...], (((1,), (1,)), ((), ())), preferred_element_type=F32
        ).astype(BF16)
    store(out_ref, out_hbm)
    for group in range(owners // 8):
        grads = lax.dot_general(
            adj_ref[:, 256 * group : 256 * group + 256],
            grads_ref[...],
            (((0,), (0,)), ((), ())),
            preferred_element_type=F32,
        )
        for step in range(8):
            owner = 8 * group + step
            one = jnp.where(slot < counts_ref[0, owner], grads[slots * step : slots * step + slots], 0.0)
            for part in range(4):
                packed_ref[owner * 4 + part] = pack_pair(one[:16], one[16:], part).astype(BF16)
        at = pl.ds(32 * group, 32)
        store(packed_ref.at[at], messages_hbm.at[at])
    part_ref[...] = lax.dot_general(
        agg_ref[...], grad_pre_ref[...], (((0,), (0,)), ((), ())), preferred_element_type=F32
    )
    store(part_ref, part_hbm)
    adj_local_in.wait()
    for at in chunks:
        sums_ref[at, :] = lax.dot_general(
            adj_local_ref[:, at], grads_ref[...], (((0,), (0,)), ((), ())), preferred_element_type=F32
        )
    for rep in range(4):

        @pl.when(rep_ref[0] == rep)
        def _(rep=rep):
            for base in range(0, half, 128):
                first, second = sums_ref[base : base + 128, :], sums_ref[half + base : half + base + 128, :]
                for part in range(4):
                    parts_ref[part ^ rep, base : base + 128, :] = pack_pair(first, second, part).astype(BF16)

    for i, local_hbm in enumerate(local_hbms):
        store(parts_ref.at[i], local_hbm)
    for copy in stores:
        copy.wait()


def add_rows(total, high, columns, second, packed):
    row = lax.broadcasted_iota(I32, (512, 128), 0)
    left = lax.broadcasted_iota(I32, (128, 128), 1) < 64
    group = jnp.where(left, 0, 1)
    blocks = packed.shape[0] // 128
    picks, spread = [[], []], [[], []]
    for i in range(blocks):
        wide = packed[128 * i : 128 * i + 128, :].astype(F32)
        turned = pltpu.roll(wide, 64, 1)
        for side, rows in enumerate((jnp.where(left, wide, turned), jnp.where(left, turned, wide))):
            at = i + second * side
            low = spread_column(columns, at)
            spread[side].append(
                jnp.concatenate(
                    [jnp.where(low == group, rows, 0.0), jnp.where(low == group + 2, rows, 0.0)], 1
                ).astype(BF16)
            )
            picks[side].append(jnp.where(row == high[at : at + 1, :], 1.0, 0.0).astype(BF16))
    return total + jnp.dot(
        jnp.concatenate(picks[0] + picks[1], 1),
        jnp.concatenate(spread[0] + spread[1], 0),
        preferred_element_type=F32,
    )


def scatter_local_kernel(ids_ref, *refs):
    packed_refs, out_ref = refs[:4], refs[4]
    ids = ids_ref[...]
    high, columns = ids & 511, (ids >> 9).T
    total = jnp.zeros((512, 256), F32)
    for i, packed_ref in enumerate(packed_refs):
        total = add_rows(total, high[4 * i :], columns[:, 4 * i :], 16, packed_ref[...])
    out_ref[...] = total


def scatter_halo_kernel(ids_ref, packed_ref, start_ref, out_ref):
    ids = ids_ref[...]
    high, columns = ids & 511, (ids >> 9).T
    total = start_ref[...]
    for i in range(4):
        packed = packed_ref[1024 * i : 1024 * i + 1024, :]
        total = add_rows(total, high[8 * i :], columns[:, 8 * i :], 32, packed)
    out_ref[...] = total.astype(BF16)


def unpack_kernel(rep_ref, *refs):
    tables, out_ref = refs[:4], refs[4]
    left = lax.broadcasted_iota(I32, (128, 128), 1) < 64
    for rep in range(4):

        @pl.when(rep_ref[0] == rep)
        def _(rep=rep):
            for low in range(4):
                for base in range(0, 512, 128):
                    block = [
                        tables[(rep - part) % 4][base : base + 128, 128 * (low // 2) : 128 * (low // 2) + 128].astype(F32)
                        for part in range(4)
                    ]
                    for pair in range(2):
                        one, two = block[2 * pair], block[2 * pair + 1]
                        if low % 2 == 0:
                            joined = jnp.where(left, one, pltpu.roll(two, 64, 1))
                        else:
                            joined = jnp.where(left, pltpu.roll(one, 64, 1), two)
                        out_ref[512 * low + base : 512 * low + base + 128, 128 * pair : 128 * pair + 128] = joined


def exchange(x, axes):
    return lax.all_to_all(x, axes, split_axis=0, concat_axis=0, tiled=True)


def from_behind(x, by):
    return lax.ppermute(x, "rep", [(i, (i + by) % 4) for i in range(4)])


def rows_of(x, index, rows):
    return lax.dynamic_slice_in_dim(x, index * rows, rows, 0)


def swap(x, axis, bit):
    return lax.ppermute(x, axis, [(i, i ^ bit) for i in range(lax.axis_size(axis))])


HALVES = (("dom", 1), ("dom", 2), ("dom", 4), ("rep", 1), ("rep", 2))


def sum_share(part):
    for axis, bit in HALVES:
        mine = jnp.where(lax.axis_index(axis) & bit != 0, 1, 0)
        rows = part.shape[0] // 2
        part = rows_of(part, mine, rows) + swap(rows_of(part, 1 - mine, rows), axis, bit)
    for bit in (8, 16, 32):
        part = part + swap(part, "dom", bit)
    return part


def joined(part, other, upper):
    return jnp.where(upper, jnp.concatenate([other, part], 0), jnp.concatenate([part, other], 0))


def gather_shares(part):
    for axis, bit in HALVES[::-1]:
        part = joined(part, swap(part, axis, bit), lax.axis_index(axis) & bit != 0)
    return part


def body(history, batch_ids, halo_ids, halo_counts, adj_local, adj_halo, weight, cotangent):
    owners = lax.axis_size("dom")
    replicas = lax.axis_size("rep")
    rep = lax.axis_index("rep")
    batch_rows = batch_ids.shape[0]
    slots = halo_ids.shape[2]
    width = history.shape[1]
    both = ("dom", "rep")

    asked = exchange(halo_ids.reshape(owners, 1, slots), "dom").reshape(owners, slots)
    fetched = gather_rows(history, asked)
    halo_rows = exchange(fetched.reshape(owners, slots, width), "dom").reshape(owners * slots, width)

    near = batch_ids.reshape(1, 2, batch_rows // 2)
    far = asked.reshape(1, owners, 2, slots // 2)
    for bit in (1, 2):
        both_ids = jnp.concatenate([near.reshape(-1), far.reshape(-1)]).reshape(-1, 128)
        other = swap(both_ids, "rep", bit).reshape(-1)
        near = jnp.concatenate([near, other[: near.size].reshape(near.shape)], 0)
        far = joined(far, other[near.size // 2 :].reshape(far.shape), rep & bit != 0)
    local_ids = near.transpose(1, 0, 2).reshape(-1, 128)
    asked_ids = far.transpose(2, 1, 0, 3).reshape(-1, 128)
    halo_rows, local_ids, asked_ids = lax.optimization_barrier((halo_rows, local_ids, asked_ids))

    inputs = gather_rows(history, batch_ids.reshape(-1, 128))
    local = jnp.dot(adj_local, inputs, preferred_element_type=F32)
    like = jax.ShapeDtypeStruct
    rep_of = rep.reshape(1)
    layer_out, weight_part, messages, *locals_ = pl.pallas_call(
        middle_kernel,
        out_shape=(
            like((batch_rows, width), BF16),
            like((width, width), F32),
            like((owners * replicas, slots // 2, 128), BF16),
        )
        + (like((batch_rows // 2, 128), BF16),) * replicas,
        in_specs=[SMEM, SMEM] + [ANY] * 6,
        out_specs=(ANY,) * (3 + replicas),
        scratch_shapes=[pltpu.VMEM(a.shape, a.dtype) for a in (halo_rows, adj_halo, local, weight, cotangent, adj_local)]
        + [
            pltpu.VMEM((batch_rows, width), BF16),
            pltpu.VMEM((width, width), F32),
            pltpu.VMEM((owners * replicas, slots // 2, 128), BF16),
            pltpu.VMEM((replicas, batch_rows // 2, 128), BF16),
            pltpu.VMEM((owners * slots, width), BF16),
            pltpu.VMEM((batch_rows, width), BF16),
            pltpu.VMEM((batch_rows, width), BF16),
            pltpu.VMEM((batch_rows, width), BF16),
            pltpu.VMEM((batch_rows, width), F32),
            pltpu.SemaphoreType.DMA((5 + batch_rows // 256,)),
            pltpu.SemaphoreType.DMA((2 + replicas + owners // 8,)),
        ],
        compiler_params=pltpu.CompilerParams(vmem_limit_bytes=56 * 1024 * 1024),
        cost_estimate=pl.CostEstimate(flops=2 * 7 * 2**20 * width, bytes_accessed=10 * 2**20, transcendentals=0),
    )(halo_counts, rep_of, halo_rows, adj_halo, local, weight, cotangent, adj_local)
    arrived = exchange(messages, both).reshape(owners * replicas * slots // 2, 128)
    weight_share = sum_share(weight_part)
    locals_ = [locals_[0]] + [swap(locals_[bits], "rep", bits) for bits in (1, 2, 3)]
    started = vmem_call(
        scatter_local_kernel,
        like((512, 256), F32),
        [VMEM] * 5,
        flops=2 * 4096 * 512 * 256,
        moved=4 * 2**20,
    )(local_ids, *locals_)
    arrived, weight_share, started = lax.optimization_barrier((arrived, weight_share, started))
    weight_sum = gather_shares(weight_share)
    table = vmem_call(
        scatter_halo_kernel,
        like((512, 256), BF16),
        [VMEM] * 3,
        flops=2 * 8192 * 512 * 256,
        moved=6 * 2**20,
    )(asked_ids, arrived, started)
    tables = [table] + [from_behind(table, by) for by in (1, 2, 3)]
    history_grad = vmem_call(
        unpack_kernel,
        like(history.shape, F32),
        [SMEM] + [VMEM] * 4,
        moved=4 * 2**20,
    )(rep_of, *tables)

    total_rows = batch_rows * owners * replicas
    grad_weight = weight_sum / jnp.sqrt(jnp.float32(total_rows))
    return (layer_out, grad_weight, history_grad)


def solution(mesh):
    return jax.shard_map(
        body,
        mesh=mesh,
        in_specs=(
            P("dom", None),
            P(("dom", "rep")),
            P(("dom", "rep"), None, None),
            P(("dom", "rep"), None),
            P(("dom", "rep"), None),
            P(("dom", "rep"), None),
            P(),
            P(("dom", "rep"), None),
        ),
        out_specs=(P(("dom", "rep"), None), P(), P("dom", None)),
        check_vma=False,
    )
```

profile of v0, /device:TPU:24, one launch (start us, length us, event | category | flops | bytes accessed | tf_op | source)
XLA Modules:
  0.0 154.3 jit_solution(13889423750537876519)
XLA Ops:
  0.6 0.8 copy.22
  1.4 21.3 %all_to_all.15 = s32[64,1,32]{2,1,0:T(1,128)S(1)} all-to-all(s32[64,1,32]{2,1,0:T(1,128)S(1)} %bitcast.27), channel_id=1, replica_groups=mesh['dom'=64,'rep'=4] {'dom'}, dimensions={0} | all-to-all | bytes 16384 | tf_op jit(solution)/shard_map/all_to_all | solution.py:222
  22.8 1.2 copy-done.1
  24.0 3.5 %shard_map.103 = bf16[2048,256]{1,0:T(8,128)(2,1)} custom-call(s32[64,32]{1,0:T(8,128)S(1)} %bitcast.24, bf16[2048,256]{1,0:T(8,128)(2,1)S(1)} %copy-done.1), custom_call_target="tpu_custom_call" | custom-call | flops 2147483648 | bytes 2097152 | tf_op jit(solution)/shard_map/pallas_call | solution.py:46
  27.4 4.8 %all-to-all-start.1 = ((bf16[64,32,256]{2,1,0:T(8,128)(2,1)}), bf16[64,32,256]{2,1,0:T(8,128)(2,1)S(1)}, u32[]{:S(2)}, u32[]{:S(2)}) async-start(bf16[64,32,256]{2,1,0:T(8,128)(2,1)} %bitcast.3), calls=%async_computation.1 | async-start | bytes 2097152 | tf_op jit(solution)/shard_map/all_to_all | solution.py:222
  32.2 0.5 broadcast.7
  32.8 0.7 reduce.3
  33.5 0.1 reshape_reshape_reshape.3
  33.6 0.8 collective-permute-start
  34.4 1.4 shard_map.104
  35.8 0.1 copy.23
  35.9 1.5 collective-permute-done
  37.3 0.1 reshape.81
  37.5 0.1 copy.24
  37.6 0.1 copy.26
  37.7 0.2 select_n.108
  37.9 1.5 collective-permute-start.1
  39.4 3.3 %convolution_bitcast_fusion.local_hbm = f32[1024,256]{1,0:T(8,128)} fusion(bf16[1024,1024]{1,0:T(8,128)(2,1)} %adj_local_hbm.1, bf16[1024,256]{1,0:T(8,128)(2,1)S(1)} %shard_map.104), kind=kOutput, calls=%fused_computation | convolution fusion | flops 536870912 | bytes 3670016 | tf_op jit(solution)/shard_map/dot_general | solution.py:285
  42.7 0.8 collective-permute-done.1
  43.5 0.2 reshape.85
  43.7 0.1 copy.28
  43.8 0.1 copy.30
  44.0 0.2 reshape.86.ids_ref
  44.3 16.9 %all-to-all-done.1 = bf16[64,32,256]{2,1,0:T(8,128)(2,1)S(1)} async-done(((bf16[64,32,256]{2,1,0:T(8,128)(2,1)}), bf16[64,32,256]{2,1,0:T(8,128)(2,1)S(1)}, u32[]{:S(2)}, u32[]{:S(2)}) %all-to-all-start.1) | async-done | bytes 1048608 | tf_op jit(solution)/shard_map/all_to_all | solution.py:222
  61.1 1.0 copy-done.4
  62.1 9.8 %shard_map.105 = (bf16[1024,256]{1,0:T(8,128)(2,1)}, f32[256,256]{1,0:T(8,128)}, bf16[256,16,128]{2,1,0:T(8,128)(2,1)}, bf16[512,128]{1,0:T(8,128)(2,1)}, bf16[5...) custom-call(s32[1,64]{1,0:T(1,128)} %counts_ref.1, s32[1]{0:T(128)} %bitcast.rep_ref, ...), custom_call_target="tpu_custom_call" | custom-call | flops 3758096384 | bytes 10485760 | tf_op jit(solution)/shard_map/pallas_call | solution.py:288
  71.9 0.0 copy-start.5
  72.0 8.1 %all-to-all-start.2 = ((bf16[256,16,128]{2,1,0:T(8,128)(2,1)}), bf16[256,16,128]{2,1,0:T(8,128)(2,1)S(1)}, u32[]{:S(2)}, u32[]{:S(2)}) async-start(bf16[256,16,128]{2,1,0:T(8,128)(2,1)} %get-tuple-element.18), calls=%async_computation.2 | async-start | bytes 2097152 | tf_op jit(solution)/shard_map/all_to_all | solution.py:222
  80.1 0.2 collective-permute-start.2
  80.3 1.2 collective-permute-done.2
  81.6 1.6 %collective-permute-start.3 = (f32[64,256]{1,0:T(8,128)S(1)}, f32[64,256]{1,0:T(8,128)S(1)}, u32[]{:S(2)}, u32[]{:S(2)}) collective-permute-start(f32[64,256]{1,0:T(8,128)S(1)} %constant_dynamic-slice_fusion.3), channel_id=1, source_target_pairs={{0,8},{4,12},{8,0},{12,4},{16,24},{20,28},{24,16},{28,20},{32,40},... | collective-permute-start | bytes 196616 | tf_op jit(solution)/shard_map/ppermute | solution.py:234
  83.1 3.8 %collective-permute-done.3 = f32[64,256]{1,0:T(8,128)S(1)} collective-permute-done((f32[64,256]{1,0:T(8,128)S(1)}, f32[64,256]{1,0:T(8,128)S(1)}, u32[]{:S(2)}, u32[]{:S(2)}) %collective-permute-start.3) | collective-permute-done | bytes 65568 | tf_op jit(solution)/shard_map/ppermute | solution.py:234
  87.0 3.7 %collective-permute-start.4 = (f32[32,256]{1,0:T(8,128)S(1)}, f32[32,256]{1,0:T(8,128)S(1)}, u32[]{:S(2)}, u32[]{:S(2)}) collective-permute-start(f32[32,256]{1,0:T(8,128)S(1)} %constant_dynamic-slice_fusion.2), channel_id=1, source_target_pairs={{0,16},{4,20},{8,24},{12,28},{16,0},{20,4},{24,8},{28,12},{32,48},... | collective-permute-start | bytes 98312 | tf_op jit(solution)/shard_map/ppermute | solution.py:234
  90.7 2.1 %collective-permute-done.4 = f32[32,256]{1,0:T(8,128)S(1)} collective-permute-done((f32[32,256]{1,0:T(8,128)S(1)}, f32[32,256]{1,0:T(8,128)S(1)}, u32[]{:S(2)}, u32[]{:S(2)}) %collective-permute-start.4) | collective-permute-done | bytes 32800 | tf_op jit(solution)/shard_map/ppermute | solution.py:234
  92.7 1.0 collective-permute-start.5
  93.7 2.9 %collective-permute-done.5 = f32[16,256]{1,0:T(8,128)S(1)} collective-permute-done((f32[16,256]{1,0:T(8,128)S(1)}, f32[16,256]{1,0:T(8,128)S(1)}, u32[]{:S(2)}, u32[]{:S(2)}) %collective-permute-start.5) | collective-permute-done | bytes 16416 | tf_op jit(solution)/shard_map/ppermute | solution.py:234
  96.6 1.7 %collective-permute-start.6 = (f32[8,256]{1,0:T(8,128)S(1)}, f32[8,256]{1,0:T(8,128)S(1)}, u32[]{:S(2)}, u32[]{:S(2)}) collective-permute-start(f32[8,256]{1,0:T(8,128)S(1)} %constant_dynamic-slice_fusion), channel_id=1, source_target_pairs={{0,2},{1,3},{2,0},{3,1},{4,6},{5,7},{6,4},{7,5},{8,10},{9,11},{10,... | collective-permute-start | bytes 24584 | tf_op jit(solution)/shard_map/ppermute | solution.py:234
  98.3 1.4 collective-permute-start.10
  99.8 2.1 %collective-permute-start.11 = (bf16[512,128]{1,0:T(8,128)(2,1)S(1)}, bf16[512,128]{1,0:T(8,128)(2,1)S(1)}, u32[]{:S(2)}, u32[]{:S(2)}) collective-permute-start(bf16[512,128]{1,0:T(8,128)(2,1)S(1)} %copy-done.7), channel_id=1, source_target_pairs={{0,2},{1,3},{2,0},{3,1},{4,6},{5,7},{6,4},{7,5},{8,10},{9,11},{10,... | collective-permute-start | bytes 393224 | tf_op jit(solution)/shard_map/ppermute | solution.py:234
  101.9 1.2 collective-permute-start.12
  103.0 1.7 %collective-permute-start.7 = (f32[8,256]{1,0:T(8,128)S(1)}, f32[8,256]{1,0:T(8,128)S(1)}, u32[]{:S(2)}, u32[]{:S(2)}) collective-permute-start(f32[8,256]{1,0:T(8,128)S(1)} %dynamic-slice_add_fusion.4), channel_id=1, source_target_pairs={{0,32},{4,36},{8,40},{12,44},{16,48},{20,52},{24,56},{28,60},{32,0... | collective-permute-start | bytes 24584 | tf_op jit(solution)/shard_map/ppermute | solution.py:234
  104.7 2.0 %collective-permute-done.7 = f32[8,256]{1,0:T(8,128)S(1)} collective-permute-done((f32[8,256]{1,0:T(8,128)S(1)}, f32[8,256]{1,0:T(8,128)S(1)}, u32[]{:S(2)}, u32[]{:S(2)}) %collective-permute-start.7) | collective-permute-done | bytes 8224 | tf_op jit(solution)/shard_map/ppermute | solution.py:234
  106.7 3.0 %collective-permute-start.8 = (f32[8,256]{1,0:T(8,128)S(1)}, f32[8,256]{1,0:T(8,128)S(1)}, u32[]{:S(2)}, u32[]{:S(2)}) collective-permute-start(f32[8,256]{1,0:T(8,128)S(1)} %add.69), channel_id=1, source_target_pairs={{0,64},{4,68},{8,72},{12,76},{16,80},{20,84},{24,88},{28,92},{32,9... | collective-permute-start | bytes 24584 | tf_op jit(solution)/shard_map/ppermute | solution.py:234
  109.7 1.6 %collective-permute-done.8 = f32[8,256]{1,0:T(8,128)S(1)} collective-permute-done((f32[8,256]{1,0:T(8,128)S(1)}, f32[8,256]{1,0:T(8,128)S(1)}, u32[]{:S(2)}, u32[]{:S(2)}) %collective-permute-start.8) | collective-permute-done | bytes 8224 | tf_op jit(solution)/shard_map/ppermute | solution.py:234
  111.3 6.5 %collective-permute-start.9 = (f32[8,256]{1,0:T(8,128)S(1)}, f32[8,256]{1,0:T(8,128)S(1)}, u32[]{:S(2)}, u32[]{:S(2)}) collective-permute-start(f32[8,256]{1,0:T(8,128)S(1)} %add.70), channel_id=1, source_target_pairs={{0,128},{4,132},{8,136},{12,140},{16,144},{20,148},{24,152},{28,15... | collective-permute-start | bytes 24584 | tf_op jit(solution)/shard_map/ppermute | solution.py:234
  117.8 1.9 %shard_map.106.start_ref = f32[512,256]{1,0:T(8,128)S(1)} custom-call(s32[32,128]{1,0:T(8,128)S(1)} %reshape.84.ids_ref, bf16[512,128]{1,0:T(8,128)(2,1)S(1)} %copy-done.3, bf16[512,128]{1,0:T(8,128)(2,1)S(1)} %collective-permute-done.10.refs_1_, bf16[512,128]{1,0:T(8,128)(2,1)S(1)} %collective-permute-done.11.refs_2_, ...), custom_call_target="tpu_custom_call" | custom-call | flops 1073741824 | bytes 4194304 | tf_op jit(solution)/shard_map/pallas_call | solution.py:318
  119.8 1.4 collective-permute-start.13
  121.2 3.8 %collective-permute-done.13 = f32[8,256]{1,0:T(8,128)S(1)} collective-permute-done((f32[8,256]{1,0:T(8,128)S(1)}, f32[8,256]{1,0:T(8,128)S(1)}, u32[]{:S(2)}, u32[]{:S(2)}) %collective-permute-start.13) | collective-permute-done | bytes 8224 | tf_op jit(solution)/shard_map/ppermute | solution.py:234
  125.0 0.9 collective-permute-start.14
  126.0 2.8 %collective-permute-done.14 = f32[16,256]{1,0:T(8,128)S(1)} collective-permute-done((f32[16,256]{1,0:T(8,128)S(1)}, f32[16,256]{1,0:T(8,128)S(1)}, u32[]{:S(2)}, u32[]{:S(2)}) %collective-permute-start.14) | collective-permute-done | bytes 16416 | tf_op jit(solution)/shard_map/ppermute | solution.py:234
  128.8 3.1 %collective-permute-start.15 = (f32[32,256]{1,0:T(8,128)S(1)}, f32[32,256]{1,0:T(8,128)S(1)}, u32[]{:S(2)}, u32[]{:S(2)}) collective-permute-start(f32[32,256]{1,0:T(8,128)S(1)} %maximum_select_fusion.3), channel_id=1, source_target_pairs={{0,16},{4,20},{8,24},{12,28},{16,0},{20,4},{24,8},{28,12},{32,48},... | collective-permute-start | bytes 98312 | tf_op jit(solution)/shard_map/ppermute | solution.py:234
  131.9 2.3 %collective-permute-done.15 = f32[32,256]{1,0:T(8,128)S(1)} collective-permute-done((f32[32,256]{1,0:T(8,128)S(1)}, f32[32,256]{1,0:T(8,128)S(1)}, u32[]{:S(2)}, u32[]{:S(2)}) %collective-permute-start.15) | collective-permute-done | bytes 32800 | tf_op jit(solution)/shard_map/ppermute | solution.py:234
  134.2 2.1 %collective-permute-start.16 = (f32[64,256]{1,0:T(8,128)S(1)}, f32[64,256]{1,0:T(8,128)S(1)}, u32[]{:S(2)}, u32[]{:S(2)}) collective-permute-start(f32[64,256]{1,0:T(8,128)S(1)} %maximum_select_fusion.2), channel_id=1, source_target_pairs={{0,8},{4,12},{8,0},{12,4},{16,24},{20,28},{24,16},{28,20},{32,40},... | collective-permute-start | bytes 196616 | tf_op jit(solution)/shard_map/ppermute | solution.py:234
  136.3 3.2 %shard_map.107.refs_0_ = bf16[512,256]{1,0:T(8,128)(2,1)S(1)} custom-call(s32[64,128]{1,0:T(8,128)S(1)} %reshape.86.ids_ref, bf16[4096,128]{1,0:T(8,128)(2,1)S(1)} %bitcast.23, f32[512,256]{1,0:T(8,128)S(1)} %shard_map.106.start_ref), custom_call_target="tpu_custom_call" | custom-call | flops 2147483648 | bytes 6291456 | tf_op jit(solution)/shard_map/pallas_call | solution.py:327
  139.5 2.7 %collective-permute-start.18 = (bf16[512,256]{1,0:T(8,128)(2,1)S(1)}, bf16[512,256]{1,0:T(8,128)(2,1)S(1)}, u32[]{:S(2)}, u32[]{:S(2)}) collective-permute-start(bf16[512,256]{1,0:T(8,128)(2,1)S(1)} %shard_map.107.refs_0_), channel_id=1, source_target_pairs={{0,1},{1,2},{2,3},{3,0},{4,5},{5,6},{6,7},{7,4},{8,9},{9,10},{10,1... | collective-permute-start | bytes 786440 | tf_op jit(solution)/shard_map/ppermute | solution.py:226
  142.2 0.1 collective-permute-start.19
  142.2 0.9 collective-permute-start.20
  143.1 0.1 collective-permute-start.17
  143.2 1.3 collective-permute-done.17
  144.6 0.7 fusion
  145.3 3.6 %collective-permute-done.18.refs_1_ = bf16[512,256]{1,0:T(8,128)(2,1)S(1)} collective-permute-done((bf16[512,256]{1,0:T(8,128)(2,1)S(1)}, bf16[512,256]{1,0:T(8,128)(2,1)S(1)}, u32[]{:S(2)}, u32[]{:S(2)}) %collective-permute-start.18) | collective-permute-done | bytes 262176 | tf_op jit(solution)/shard_map/ppermute | solution.py:226
  148.9 1.2 collective-permute-done.19.refs_2_
  150.1 2.5 %collective-permute-done.20.refs_3_ = bf16[512,256]{1,0:T(8,128)(2,1)S(1)} collective-permute-done((bf16[512,256]{1,0:T(8,128)(2,1)S(1)}, bf16[512,256]{1,0:T(8,128)(2,1)S(1)}, u32[]{:S(2)}, u32[]{:S(2)}) %collective-permute-start.20) | collective-permute-done | bytes 262176 | tf_op jit(solution)/shard_map/ppermute | solution.py:226
  152.6 1.7 %shard_map.108 = f32[2048,256]{1,0:T(8,128)} custom-call(s32[1]{0:T(128)} %bitcast.rep_ref, bf16[512,256]{1,0:T(8,128)(2,1)S(1)} %shard_map.107.refs_0_, bf16[512,256]{1,0:T(8,128)(2,1)S(1)} %collective-permute-done.18.refs_1_, bf16[512,256]{1,0:T(8,128)(2,1)S(1)} %collective-permute-done.19.refs_2_, bf16[512,256]{1,0:T(8,128)(2,1)S(1)} %collective-permute-done.20.refs_3_), custom_call_target="tpu_custom_call" | custom-call | bytes 4194304 | tf_op jit(solution)/shard_map/pallas_call | solution.py:335
  (55 shorter events, 0.3 us)
Async XLA Ops:
  22.8 1.2 copy-start.1
  27.4 6.1 %copy-start = (s32[1024]{0:T(1024)S(1)}, s32[1024]{0:T(1024)}, u32[]{:S(2)}) copy-start(s32[1024]{0:T(1024)} %param.9) | copy-start | bytes 12292
  27.4 7.0 %copy-start.2 = (bf16[2048,256]{1,0:T(8,128)(2,1)S(1)}, bf16[2048,256]{1,0:T(8,128)(2,1)}, u32[]{:S(2)}) copy-start(bf16[2048,256]{1,0:T(8,128)(2,1)} %table_ref.3) | copy-start | bytes 3145732
  27.4 33.7 %all-to-all-start.1 = ((bf16[64,32,256]{2,1,0:T(8,128)(2,1)}), bf16[64,32,256]{2,1,0:T(8,128)(2,1)S(1)}, u32[]{:S(2)}, u32[]{:S(2)}) async-start(bf16[64,32,256]{2,1,0:T(8,128)(2,1)} %bitcast.3), calls=%async_computation.1 | async-start | bytes 2097152 | tf_op jit(solution)/shard_map/all_to_all | solution.py:222
  33.6 3.8 %collective-permute-start = (s32[24,128]{1,0:T(8,128)S(1)}, s32[24,128]{1,0:T(8,128)S(1)}, u32[]{:S(2)}, u32[]{:S(2)}) collective-permute-start(s32[24,128]{1,0:T(8,128)S(1)} %add_bitcast_fusion.2), channel_id=1, source_target_pairs={{0,1},{1,0},{2,3},{3,2},{4,5},{5,4},{6,7},{7,6},{8,9},{9,8},{10,11... | collective-permute-start | bytes 36872 | tf_op jit(solution)/shard_map/ppermute | solution.py:234
  37.9 5.6 %collective-permute-start.1 = (s32[48,128]{1,0:T(8,128)S(1)}, s32[48,128]{1,0:T(8,128)S(1)}, u32[]{:S(2)}, u32[]{:S(2)}) collective-permute-start(s32[48,128]{1,0:T(8,128)S(1)} %add_bitcast_fusion), channel_id=1, source_target_pairs={{0,2},{1,3},{2,0},{3,1},{4,6},{5,7},{6,4},{7,5},{8,10},{9,11},{10,... | collective-permute-start | bytes 73736 | tf_op jit(solution)/shard_map/ppermute | solution.py:234
  61.1 1.0 copy-start.4
  71.9 8.1 %copy-start.5 = (f32[256,256]{1,0:T(8,128)S(1)}, f32[256,256]{1,0:T(8,128)}, u32[]{:S(2)}) copy-start(f32[256,256]{1,0:T(8,128)} %get-tuple-element.19) | copy-start | bytes 786436
  72.0 26.4 %copy-start.8 = (bf16[512,128]{1,0:T(8,128)(2,1)S(1)}, bf16[512,128]{1,0:T(8,128)(2,1)}, u32[]{:S(2)}) copy-start(bf16[512,128]{1,0:T(8,128)(2,1)} %get-tuple-element.22) | copy-start | bytes 393220
  72.0 27.8 %copy-start.7 = (bf16[512,128]{1,0:T(8,128)(2,1)S(1)}, bf16[512,128]{1,0:T(8,128)(2,1)}, u32[]{:S(2)}) copy-start(bf16[512,128]{1,0:T(8,128)(2,1)} %get-tuple-element.23) | copy-start | bytes 393220
  72.0 29.9 %copy-start.6 = (bf16[512,128]{1,0:T(8,128)(2,1)S(1)}, bf16[512,128]{1,0:T(8,128)(2,1)}, u32[]{:S(2)}) copy-start(bf16[512,128]{1,0:T(8,128)(2,1)} %get-tuple-element.24) | copy-start | bytes 393220
  72.0 45.9 %copy-start.3 = (bf16[512,128]{1,0:T(8,128)(2,1)S(1)}, bf16[512,128]{1,0:T(8,128)(2,1)}, u32[]{:S(2)}) copy-start(bf16[512,128]{1,0:T(8,128)(2,1)} %get-tuple-element.21.refs_0_) | copy-start | bytes 393220
  72.0 47.8 %all-to-all-start.2 = ((bf16[256,16,128]{2,1,0:T(8,128)(2,1)}), bf16[256,16,128]{2,1,0:T(8,128)(2,1)S(1)}, u32[]{:S(2)}, u32[]{:S(2)}) async-start(bf16[256,16,128]{2,1,0:T(8,128)(2,1)} %get-tuple-element.18), calls=%async_computation.2 | async-start | bytes 2097152 | tf_op jit(solution)/shard_map/all_to_all | solution.py:222
  80.1 1.4 collective-permute-start.2
  81.6 5.4 %collective-permute-start.3 = (f32[64,256]{1,0:T(8,128)S(1)}, f32[64,256]{1,0:T(8,128)S(1)}, u32[]{:S(2)}, u32[]{:S(2)}) collective-permute-start(f32[64,256]{1,0:T(8,128)S(1)} %constant_dynamic-slice_fusion.3), channel_id=1, source_target_pairs={{0,8},{4,12},{8,0},{12,4},{16,24},{20,28},{24,16},{28,20},{32,40},... | collective-permute-start | bytes 196616 | tf_op jit(solution)/shard_map/ppermute | solution.py:234
  87.0 5.7 %collective-permute-start.4 = (f32[32,256]{1,0:T(8,128)S(1)}, f32[32,256]{1,0:T(8,128)S(1)}, u32[]{:S(2)}, u32[]{:S(2)}) collective-permute-start(f32[32,256]{1,0:T(8,128)S(1)} %constant_dynamic-slice_fusion.2), channel_id=1, source_target_pairs={{0,16},{4,20},{8,24},{12,28},{16,0},{20,4},{24,8},{28,12},{32,48},... | collective-permute-start | bytes 98312 | tf_op jit(solution)/shard_map/ppermute | solution.py:234
  92.7 3.8 %collective-permute-start.5 = (f32[16,256]{1,0:T(8,128)S(1)}, f32[16,256]{1,0:T(8,128)S(1)}, u32[]{:S(2)}, u32[]{:S(2)}) collective-permute-start(f32[16,256]{1,0:T(8,128)S(1)} %constant_dynamic-slice_fusion.1), channel_id=1, source_target_pairs={{0,1},{1,0},{2,3},{3,2},{4,5},{5,4},{6,7},{7,6},{8,9},{9,8},{10,11... | collective-permute-start | bytes 49160 | tf_op jit(solution)/shard_map/ppermute | solution.py:234
  96.6 6.4 %collective-permute-start.6 = (f32[8,256]{1,0:T(8,128)S(1)}, f32[8,256]{1,0:T(8,128)S(1)}, u32[]{:S(2)}, u32[]{:S(2)}) collective-permute-start(f32[8,256]{1,0:T(8,128)S(1)} %constant_dynamic-slice_fusion), channel_id=1, source_target_pairs={{0,2},{1,3},{2,0},{3,1},{4,6},{5,7},{6,4},{7,5},{8,10},{9,11},{10,... | collective-permute-start | bytes 24584 | tf_op jit(solution)/shard_map/ppermute | solution.py:234
  98.3 19.5 %collective-permute-start.10 = (bf16[512,128]{1,0:T(8,128)(2,1)S(1)}, bf16[512,128]{1,0:T(8,128)(2,1)S(1)}, u32[]{:S(2)}, u32[]{:S(2)}) collective-permute-start(bf16[512,128]{1,0:T(8,128)(2,1)S(1)} %copy-done.8), channel_id=1, source_target_pairs={{0,1},{1,0},{2,3},{3,2},{4,5},{5,4},{6,7},{7,6},{8,9},{9,8},{10,11... | collective-permute-start | bytes 393224 | tf_op jit(solution)/shard_map/ppermute | solution.py:234
  99.8 18.1 %collective-permute-start.11 = (bf16[512,128]{1,0:T(8,128)(2,1)S(1)}, bf16[512,128]{1,0:T(8,128)(2,1)S(1)}, u32[]{:S(2)}, u32[]{:S(2)}) collective-permute-start(bf16[512,128]{1,0:T(8,128)(2,1)S(1)} %copy-done.7), channel_id=1, source_target_pairs={{0,2},{1,3},{2,0},{3,1},{4,6},{5,7},{6,4},{7,5},{8,10},{9,11},{10,... | collective-permute-start | bytes 393224 | tf_op jit(solution)/shard_map/ppermute | solution.py:234
  101.9 16.0 %collective-permute-start.12 = (bf16[512,128]{1,0:T(8,128)(2,1)S(1)}, bf16[512,128]{1,0:T(8,128)(2,1)S(1)}, u32[]{:S(2)}, u32[]{:S(2)}) collective-permute-start(bf16[512,128]{1,0:T(8,128)(2,1)S(1)} %copy-done.6), channel_id=1, source_target_pairs={{0,3},{1,2},{2,1},{3,0},{4,7},{5,6},{6,5},{7,4},{8,11},{9,10},{10,... | collective-permute-start | bytes 393224 | tf_op jit(solution)/shard_map/ppermute | solution.py:234
  103.0 3.7 %collective-permute-start.7 = (f32[8,256]{1,0:T(8,128)S(1)}, f32[8,256]{1,0:T(8,128)S(1)}, u32[]{:S(2)}, u32[]{:S(2)}) collective-permute-start(f32[8,256]{1,0:T(8,128)S(1)} %dynamic-slice_add_fusion.4), channel_id=1, source_target_pairs={{0,32},{4,36},{8,40},{12,44},{16,48},{20,52},{24,56},{28,60},{32,0... | collective-permute-start | bytes 24584 | tf_op jit(solution)/shard_map/ppermute | solution.py:234
  106.7 4.6 %collective-permute-start.8 = (f32[8,256]{1,0:T(8,128)S(1)}, f32[8,256]{1,0:T(8,128)S(1)}, u32[]{:S(2)}, u32[]{:S(2)}) collective-permute-start(f32[8,256]{1,0:T(8,128)S(1)} %add.69), channel_id=1, source_target_pairs={{0,64},{4,68},{8,72},{12,76},{16,80},{20,84},{24,88},{28,92},{32,9... | collective-permute-start | bytes 24584 | tf_op jit(solution)/shard_map/ppermute | solution.py:234
  111.3 8.5 %collective-permute-start.9 = (f32[8,256]{1,0:T(8,128)S(1)}, f32[8,256]{1,0:T(8,128)S(1)}, u32[]{:S(2)}, u32[]{:S(2)}) collective-permute-start(f32[8,256]{1,0:T(8,128)S(1)} %add.70), channel_id=1, source_target_pairs={{0,128},{4,132},{8,136},{12,140},{16,144},{20,148},{24,152},{28,15... | collective-permute-start | bytes 24584 | tf_op jit(solution)/shard_map/ppermute | solution.py:234
  119.8 5.2 %collective-permute-start.13 = (f32[8,256]{1,0:T(8,128)S(1)}, f32[8,256]{1,0:T(8,128)S(1)}, u32[]{:S(2)}, u32[]{:S(2)}) collective-permute-start(f32[8,256]{1,0:T(8,128)S(1)} %add.71), channel_id=1, source_target_pairs={{0,2},{1,3},{2,0},{3,1},{4,6},{5,7},{6,4},{7,5},{8,10},{9,11},{10,... | collective-permute-start | bytes 24584 | tf_op jit(solution)/shard_map/ppermute | solution.py:234
  125.0 3.7 %collective-permute-start.14 = (f32[16,256]{1,0:T(8,128)S(1)}, f32[16,256]{1,0:T(8,128)S(1)}, u32[]{:S(2)}, u32[]{:S(2)}) collective-permute-start(f32[16,256]{1,0:T(8,128)S(1)} %maximum_select_fusion.4), channel_id=1, source_target_pairs={{0,1},{1,0},{2,3},{3,2},{4,5},{5,4},{6,7},{7,6},{8,9},{9,8},{10,11... | collective-permute-start | bytes 49160 | tf_op jit(solution)/shard_map/ppermute | solution.py:234
  128.8 5.4 %collective-permute-start.15 = (f32[32,256]{1,0:T(8,128)S(1)}, f32[32,256]{1,0:T(8,128)S(1)}, u32[]{:S(2)}, u32[]{:S(2)}) collective-permute-start(f32[32,256]{1,0:T(8,128)S(1)} %maximum_select_fusion.3), channel_id=1, source_target_pairs={{0,16},{4,20},{8,24},{12,28},{16,0},{20,4},{24,8},{28,12},{32,48},... | collective-permute-start | bytes 98312 | tf_op jit(solution)/shard_map/ppermute | solution.py:234
  134.2 8.9 %collective-permute-start.16 = (f32[64,256]{1,0:T(8,128)S(1)}, f32[64,256]{1,0:T(8,128)S(1)}, u32[]{:S(2)}, u32[]{:S(2)}) collective-permute-start(f32[64,256]{1,0:T(8,128)S(1)} %maximum_select_fusion.2), channel_id=1, source_target_pairs={{0,8},{4,12},{8,0},{12,4},{16,24},{20,28},{24,16},{28,20},{32,40},... | collective-permute-start | bytes 196616 | tf_op jit(solution)/shard_map/ppermute | solution.py:234
  139.5 9.4 %collective-permute-start.18 = (bf16[512,256]{1,0:T(8,128)(2,1)S(1)}, bf16[512,256]{1,0:T(8,128)(2,1)S(1)}, u32[]{:S(2)}, u32[]{:S(2)}) collective-permute-start(bf16[512,256]{1,0:T(8,128)(2,1)S(1)} %shard_map.107.refs_0_), channel_id=1, source_target_pairs={{0,1},{1,2},{2,3},{3,0},{4,5},{5,6},{6,7},{7,4},{8,9},{9,10},{10,1... | collective-permute-start | bytes 786440 | tf_op jit(solution)/shard_map/ppermute | solution.py:226
  142.2 8.0 %collective-permute-start.19 = (bf16[512,256]{1,0:T(8,128)(2,1)S(1)}, bf16[512,256]{1,0:T(8,128)(2,1)S(1)}, u32[]{:S(2)}, u32[]{:S(2)}) collective-permute-start(bf16[512,256]{1,0:T(8,128)(2,1)S(1)} %shard_map.107.refs_0_), channel_id=1, source_target_pairs={{0,2},{1,3},{2,0},{3,1},{4,6},{5,7},{6,4},{7,5},{8,10},{9,11},{10,... | collective-permute-start | bytes 786440 | tf_op jit(solution)/shard_map/ppermute | solution.py:226
  142.2 10.4 %collective-permute-start.20 = (bf16[512,256]{1,0:T(8,128)(2,1)S(1)}, bf16[512,256]{1,0:T(8,128)(2,1)S(1)}, u32[]{:S(2)}, u32[]{:S(2)}) collective-permute-start(bf16[512,256]{1,0:T(8,128)(2,1)S(1)} %shard_map.107.refs_0_), channel_id=1, source_target_pairs={{0,3},{1,0},{2,1},{3,2},{4,7},{5,4},{6,5},{7,6},{8,11},{9,8},{10,9... | collective-permute-start | bytes 786440 | tf_op jit(solution)/shard_map/ppermute | solution.py:226
  143.1 1.4 collective-permute-start.17
where the time goes:
time: 155 us; the launch traced here: 154 us
  starting transfers between devices  50.5 us (33%)
  waiting for transfers between devices  50.3 us (32%)
  Pallas kernels  21.4 us (14%)
  blocking collectives  21.3 us (14%)
  local copies, waits for them, and re-layouts  4.93 us (3%)
  matrix products  3.28 us (2%)
  other arithmetic  1.58 us (1%)
    ppermute x18, starting transfers between devices, swap(): lax.ppermute(x, axis, [(i, i ^ bit) for i in range(lax.axis_size(axis))])  34.1 us
    ppermute x18, waiting for transfers between devices, swap(): lax.ppermute(x, axis, [(i, i ^ bit) for i in range(lax.axis_size(axis))])  26.1 us
    all_to_all x1, blocking collectives, exchange(): return lax.all_to_all(x, axes, split_axis=0, concat_axis=0, tiled=True)  21.3 us
    all_to_all x2, waiting for transfers between devices, exchange(): return lax.all_to_all(x, axes, split_axis=0, concat_axis=0, tiled=True)  16.9 us
    all_to_all x2, starting transfers between devices, exchange(): return lax.all_to_all(x, axes, split_axis=0, concat_axis=0, tiled=True)  12.8 us
    pallas_call x1, Pallas kernels, body(): pl.pallas_call(middle_kernel, out_shape=(like((batch_rows, width), BF16),...  9.83 us
    ppermute x3, waiting for transfers between devices, from_behind(): return lax.ppermute(x, 'rep', [(i, (i + by) % 4) for i in range(4)])  7.31 us
    pallas_call x2, Pallas kernels, gather_rows(): vmem_call(gather_kernel, jax.ShapeDtypeStruct((count, width), BF16), [VME...  4.85 us
  transfers between devices with their start and end apart: 23, of which 16 were waited for; matrix products, arithmetic and copies ran while one was open for 4% of the time, Pallas kernels for 4%

commit v1 on v0

--- a/solution.py
+++ b/solution.py
@@ -8,17 +8,17 @@
 BF16, F32, I32 = jnp.bfloat16, jnp.float32, jnp.int32
 VMEM = pl.BlockSpec(memory_space=pltpu.VMEM)
 SMEM = pl.BlockSpec(memory_space=pltpu.SMEM)
-ANY = pl.BlockSpec(memory_space=pl.ANY)
-
-
-def vmem_call(kernel, out_shape, in_specs, flops=0, moved=0, scratch=()):
+ANY = pl.BlockSpec(memory_space=pltpu.HBM)
+
+
+def vmem_call(kernel, out_shape, in_specs, flops=0, moved=0, scratch=(), mib=16):
     return pl.pallas_call(
         kernel,
         out_shape=out_shape,
         in_specs=in_specs,
         out_specs=jax.tree.map(lambda _: VMEM, out_shape),
         scratch_shapes=list(scratch),
-        compiler_params=pltpu.CompilerParams(vmem_limit_bytes=16 * 1024 * 1024),
+        compiler_params=pltpu.CompilerParams(vmem_limit_bytes=mib * 2**20),
         cost_estimate=pl.CostEstimate(flops=flops, bytes_accessed=moved, transcendentals=0),
     )
 
@@ -61,11 +61,11 @@
 
 
 def middle_kernel(
-    counts_ref, rep_ref, rows_hbm, adj_hbm, local_hbm, weight_hbm, cotangent_hbm, adj_local_hbm,
+    counts_hbm, rows_ref, adj_hbm, local_hbm, weight_hbm, cotangent_hbm, adj_local_hbm,
     out_hbm, part_hbm, messages_hbm, *refs,
 ):
     local_hbms, refs = refs[:4], refs[4:]
-    rows_ref, adj_ref, local_ref, weight_ref, cotangent_ref, adj_local_ref, *refs = refs
+    counts_ref, adj_ref, local_ref, weight_ref, cotangent_ref, adj_local_ref, *refs = refs
     out_ref, part_ref, packed_ref, parts_ref, live_ref, agg_ref, grad_pre_ref, grads_ref, sums_ref, load_sems, store_sems = refs
     slots, owners = 32, 64
     half = sums_ref.shape[0] // 2
@@ -82,7 +82,7 @@
         stores.append(pltpu.make_async_copy(source, target, store_sems.at[len(stores)]))
         stores[-1].start()
 
-    rows_in = load(rows_hbm, rows_ref)
+    counts_in = load(counts_hbm, counts_ref)
     adj_in = [load(adj_hbm.at[chunks[0]], adj_ref.at[chunks[0]])]
     weight_in, local_in = load(weight_hbm, weight_ref), load(local_hbm, local_ref)
     cotangent_in = load(cotangent_hbm, cotangent_ref)
@@ -90,7 +90,7 @@
     adj_local_in = load(adj_local_hbm, adj_local_ref)
 
     slot = lax.broadcasted_iota(I32, (slots, 256), 0)
-    rows_in.wait()
+    counts_in.wait()
     for owner in range(owners):
         at = slice(slots * owner, slots * owner + slots)
         live = jnp.where(slot < counts_ref[0, owner], rows_ref[at, :].astype(F32), 0.0)
@@ -138,7 +138,7 @@
         )
     for rep in range(4):
 
-        @pl.when(rep_ref[0] == rep)
+        @pl.when(lax.axis_index("rep") == rep)
         def _(rep=rep):
             for base in range(0, half, 128):
                 first, second = sums_ref[base : base + 128, :], sums_ref[half + base : half + base + 128, :]
@@ -182,7 +182,7 @@
     high, columns = ids & 511, (ids >> 9).T
     total = jnp.zeros((512, 256), F32)
     for i, packed_ref in enumerate(packed_refs):
-        total = add_rows(total, high[4 * i :], columns[:, 4 * i :], 16, packed_ref[...])
+        total = add_rows(total, high[4 * i :], columns[:, 4 * i :], 16, packed_ref[0:512, :])
     out_ref[...] = total
 
 
@@ -196,12 +196,12 @@
     out_ref[...] = total.astype(BF16)
 
 
-def unpack_kernel(rep_ref, *refs):
+def unpack_kernel(*refs):
     tables, out_ref = refs[:4], refs[4]
     left = lax.broadcasted_iota(I32, (128, 128), 1) < 64
     for rep in range(4):
 
-        @pl.when(rep_ref[0] == rep)
+        @pl.when(lax.axis_index("rep") == rep)
         def _(rep=rep):
             for low in range(4):
                 for base in range(0, 512, 128):
@@ -234,15 +234,23 @@
     return lax.ppermute(x, axis, [(i, i ^ bit) for i in range(lax.axis_size(axis))])
 
 
-HALVES = (("dom", 1), ("dom", 2), ("dom", 4), ("rep", 1), ("rep", 2))
-
-
-def sum_share(part):
-    for axis, bit in HALVES:
-        mine = jnp.where(lax.axis_index(axis) & bit != 0, 1, 0)
-        rows = part.shape[0] // 2
-        part = rows_of(part, mine, rows) + swap(rows_of(part, 1 - mine, rows), axis, bit)
-    for bit in (8, 16, 32):
+def place(axis, bits):
+    return lax.axis_index(axis) & bits
+
+
+def sum_chip_row(part):
+    core, x = place("dom", 1), place("dom", 6) >> 1
+    part = rows_of(part, core, 128) + swap(rows_of(part, 1 - core, 128), "dom", 1)
+    return rows_of(part, x, 32) + sum(swap(rows_of(part, x ^ bits, 32), "dom", 2 * bits) for bits in (1, 2, 3))
+
+
+def sum_replicas(part):
+    others = [swap(part, "rep", bits) for bits in (1, 2, 3)]
+    return (part + others[0]) + (others[1] + others[2])
+
+
+def sum_z(part, bits):
+    for bit in bits:
         part = part + swap(part, "dom", bit)
     return part
 
@@ -251,10 +259,11 @@
     return jnp.where(upper, jnp.concatenate([other, part], 0), jnp.concatenate([part, other], 0))
 
 
-def gather_shares(part):
-    for axis, bit in HALVES[::-1]:
-        part = joined(part, swap(part, axis, bit), lax.axis_index(axis) & bit != 0)
-    return part
+def gather_chip_row(part):
+    near = [part] + [swap(part, "dom", 2 * bits) for bits in (1, 2, 3)]
+    odd, high = place("dom", 2) != 0, place("dom", 4) != 0
+    half = joined(joined(near[0], near[1], odd), joined(near[2], near[3], odd), high)
+    return joined(half, swap(half, "dom", 1), place("dom", 1) != 0)
 
 
 def body(history, batch_ids, halo_ids, halo_counts, adj_local, adj_halo, weight, cotangent):
@@ -284,7 +293,6 @@
     inputs = gather_rows(history, batch_ids.reshape(-1, 128))
     local = jnp.dot(adj_local, inputs, preferred_element_type=F32)
     like = jax.ShapeDtypeStruct
-    rep_of = rep.reshape(1)
     layer_out, weight_part, messages, *locals_ = pl.pallas_call(
         middle_kernel,
         out_shape=(
@@ -293,9 +301,10 @@
             like((owners * replicas, slots // 2, 128), BF16),
         )
         + (like((batch_rows // 2, 128), BF16),) * replicas,
-        in_specs=[SMEM, SMEM] + [ANY] * 6,
+        in_specs=[ANY, VMEM] + [ANY] * 5,
         out_specs=(ANY,) * (3 + replicas),
-        scratch_shapes=[pltpu.VMEM(a.shape, a.dtype) for a in (halo_rows, adj_halo, local, weight, cotangent, adj_local)]
+        scratch_shapes=[pltpu.SMEM(halo_counts.shape, I32)]
+        + [pltpu.VMEM(a.shape, a.dtype) for a in (adj_halo, local, weight, cotangent, adj_local)]
         + [
             pltpu.VMEM((batch_rows, width), BF16),
             pltpu.VMEM((width, width), F32),
@@ -309,21 +318,19 @@
             pltpu.SemaphoreType.DMA((5 + batch_rows // 256,)),
             pltpu.SemaphoreType.DMA((2 + replicas + owners // 8,)),
         ],
-        compiler_params=pltpu.CompilerParams(vmem_limit_bytes=56 * 1024 * 1024),
+        compiler_params=pltpu.CompilerParams(vmem_limit_bytes=56 * 2**20),
         cost_estimate=pl.CostEstimate(flops=2 * 7 * 2**20 * width, bytes_accessed=10 * 2**20, transcendentals=0),
-    )(halo_counts, rep_of, halo_rows, adj_halo, local, weight, cotangent, adj_local)
+    )(halo_counts, halo_rows, adj_halo, local, weight, cotangent, adj_local)
     arrived = exchange(messages, both).reshape(owners * replicas * slots // 2, 128)
-    weight_share = sum_share(weight_part)
+    weight_share = sum_z(sum_replicas(sum_chip_row(weight_part)), (8, 16))
     locals_ = [locals_[0]] + [swap(locals_[bits], "rep", bits) for bits in (1, 2, 3)]
     started = vmem_call(
         scatter_local_kernel,
         like((512, 256), F32),
         [VMEM] * 5,
-        flops=2 * 4096 * 512 * 256,
-        moved=4 * 2**20,
+        moved=2**17,
     )(local_ids, *locals_)
-    arrived, weight_share, started = lax.optimization_barrier((arrived, weight_share, started))
-    weight_sum = gather_shares(weight_share)
+    arrived, started, weight_share = lax.optimization_barrier((arrived, started, weight_share))
     table = vmem_call(
         scatter_halo_kernel,
         like((512, 256), BF16),
@@ -331,13 +338,16 @@
         flops=2 * 8192 * 512 * 256,
         moved=6 * 2**20,
     )(asked_ids, arrived, started)
+    weight_share = sum_z(weight_share, (32,))
+    table, weight_share = lax.optimization_barrier((table, weight_share))
+    weight_sum = gather_chip_row(sum_z(weight_share, ()))
     tables = [table] + [from_behind(table, by) for by in (1, 2, 3)]
     history_grad = vmem_call(
         unpack_kernel,
         like(history.shape, F32),
-        [SMEM] + [VMEM] * 4,
+        [VMEM] * 4,
         moved=4 * 2**20,
-    )(rep_of, *tables)
+    )(*tables)
 
     total_rows = batch_rows * owners * replicas
     grad_weight = weight_sum / jnp.sqrt(jnp.float32(total_rows))

time: 155 us -> 139 us (0.90)
  the two profiles are of different devices: /device:TPU:24 before, /device:TPU:1 now
where the time goes in v1:
time: 139 us; the launch traced here: 138 us
  starting transfers between devices  51.2 us (37%)
  waiting for transfers between devices  32.4 us (23%)
  blocking collectives  22.2 us (16%)
  Pallas kernels  21.7 us (16%)
  local copies, waits for them, and re-layouts  4.91 us (4%)
  matrix products  3.29 us (2%)
  other arithmetic  1.59 us (1%)
    ppermute x19, starting transfers between devices, swap(): lax.ppermute(x, axis, [(i, i ^ bit) for i in range(lax.axis_size(axis))])  33.5 us
    all_to_all x1, blocking collectives, exchange(): return lax.all_to_all(x, axes, split_axis=0, concat_axis=0, tiled=True)  22.2 us
    all_to_all x2, waiting for transfers between devices, exchange(): return lax.all_to_all(x, axes, split_axis=0, concat_axis=0, tiled=True)  17.5 us
    ppermute x19, waiting for transfers between devices, swap(): lax.ppermute(x, axis, [(i, i ^ bit) for i in range(lax.axis_size(axis))])  14.9 us
    all_to_all x2, starting transfers between devices, exchange(): return lax.all_to_all(x, axes, split_axis=0, concat_axis=0, tiled=True)  14 us
    pallas_call x1, Pallas kernels, body(): pl.pallas_call(middle_kernel, out_shape=(like((batch_rows, width), BF16),...  10.1 us
    pallas_call x2, Pallas kernels, gather_rows(): vmem_call(gather_kernel, jax.ShapeDtypeStruct((count, width), BF16), [VME...  4.85 us
    ppermute x3, starting transfers between devices, from_behind(): return lax.ppermute(x, 'rep', [(i, (i + by) % 4) for i in range(4)])  3.74 us
  transfers between devices with their start and end apart: 24, of which 11 were waited for; matrix products, arithmetic and copies ran while one was open for 5% of the time, Pallas kernels for 5%

profile of v1, /device:TPU:1, one launch (start us, length us, event | category | flops | bytes accessed | tf_op | source)
XLA Modules:
  0.0 138.2 jit_solution(12633268731021473364)
XLA Ops:
  0.6 0.8 copy.22
  1.4 22.2 %all_to_all.15 = s32[64,1,32]{2,1,0:T(1,128)S(1)} all-to-all(s32[64,1,32]{2,1,0:T(1,128)S(1)} %bitcast.26), channel_id=1, replica_groups=mesh['dom'=64,'rep'=4] {'dom'}, dimensions={0} | all-to-all | bytes 16384 | tf_op jit(solution)/shard_map/all_to_all | solution.py:222
  23.6 1.2 copy-done.2
  24.8 3.5 %shard_map.103 = bf16[2048,256]{1,0:T(8,128)(2,1)} custom-call(s32[64,32]{1,0:T(8,128)S(1)} %bitcast.23, bf16[2048,256]{1,0:T(8,128)(2,1)S(1)} %copy-done.2), custom_call_target="tpu_custom_call" | custom-call | flops 2147483648 | bytes 2097152 | tf_op jit(solution)/shard_map/pallas_call | solution.py:46
  28.3 4.9 %all-to-all-start.1 = ((bf16[64,32,256]{2,1,0:T(8,128)(2,1)}), bf16[64,32,256]{2,1,0:T(8,128)(2,1)S(1)}, u32[]{:S(2)}, u32[]{:S(2)}) async-start(bf16[64,32,256]{2,1,0:T(8,128)(2,1)} %bitcast.2), calls=%async_computation.1 | async-start | bytes 2097152 | tf_op jit(solution)/shard_map/all_to_all | solution.py:222
  33.2 0.5 broadcast.7
  33.7 0.7 reduce.3
  34.4 0.1 reshape_reshape_reshape.3
  34.5 1.4 collective-permute-start
  35.9 1.4 %shard_map.104 = bf16[1024,256]{1,0:T(8,128)(2,1)S(1)} custom-call(s32[8,128]{1,0:T(8,128)S(1)} %bitcast.24, bf16[2048,256]{1,0:T(8,128)(2,1)S(1)} %copy-done.3), custom_call_target="tpu_custom_call" | custom-call | flops 1073741824 | bytes 1048576 | tf_op jit(solution)/shard_map/pallas_call | solution.py:46
  37.3 0.1 copy.23
  37.4 0.1 collective-permute-done
  37.4 0.1 reshape.77
  37.6 0.1 copy.24
  37.6 0.1 copy.26
  37.8 0.2 select_n.68
  38.0 3.2 %collective-permute-start.1 = (s32[48,128]{1,0:T(8,128)S(1)}, s32[48,128]{1,0:T(8,128)S(1)}, u32[]{:S(2)}, u32[]{:S(2)}) collective-permute-start(s32[48,128]{1,0:T(8,128)S(1)} %add_bitcast_fusion), channel_id=1, source_target_pairs={{0,2},{1,3},{2,0},{3,1},{4,6},{5,7},{6,4},{7,5},{8,10},{9,11},{10,... | collective-permute-start | bytes 73736 | tf_op jit(solution)/shard_map/ppermute | solution.py:234
  41.2 3.3 %convolution_bitcast_fusion.local_hbm = f32[1024,256]{1,0:T(8,128)} fusion(bf16[1024,1024]{1,0:T(8,128)(2,1)} %adj_local_hbm.1, bf16[1024,256]{1,0:T(8,128)(2,1)S(1)} %shard_map.104), kind=kOutput, calls=%fused_computation | convolution fusion | flops 536870912 | bytes 3670016 | tf_op jit(solution)/shard_map/dot_general | solution.py:294
  44.5 0.0 collective-permute-done.1
  44.5 0.2 reshape.81
  44.7 0.1 copy.28
  44.8 0.1 copy.30
  45.0 0.2 reshape.82.ids_ref
  45.2 16.1 %all-to-all-done.1 = bf16[64,32,256]{2,1,0:T(8,128)(2,1)S(1)} async-done(((bf16[64,32,256]{2,1,0:T(8,128)(2,1)}), bf16[64,32,256]{2,1,0:T(8,128)(2,1)S(1)}, u32[]{:S(2)}, u32[]{:S(2)}) %all-to-all-start.1) | async-done | bytes 1048608 | tf_op jit(solution)/shard_map/all_to_all | solution.py:222
  61.3 1.0 copy-done.4
  62.3 10.1 %shard_map.105 = (bf16[1024,256]{1,0:T(8,128)(2,1)}, f32[256,256]{1,0:T(8,128)}, bf16[256,16,128]{2,1,0:T(8,128)(2,1)}, bf16[512,128]{1,0:T(8,128)(2,1)}, bf16[5...) custom-call(s32[1,64]{1,0:T(1,128)} %counts_hbm.1, bf16[2048,256]{1,0:T(8,128)(2,1)} %bitcast.25, ...), custom_call_target="tpu_custom_call" | custom-call | flops 3758096384 | bytes 10485760 | tf_op jit(solution)/shard_map/pallas_call | solution.py:296
  72.4 0.0 copy-start.5
  72.4 9.1 %all-to-all-start.2 = ((bf16[256,16,128]{2,1,0:T(8,128)(2,1)}), bf16[256,16,128]{2,1,0:T(8,128)(2,1)S(1)}, u32[]{:S(2)}, u32[]{:S(2)}) async-start(bf16[256,16,128]{2,1,0:T(8,128)(2,1)} %get-tuple-element.21), calls=%async_computation.2 | async-start | bytes 2097152 | tf_op jit(solution)/shard_map/all_to_all | solution.py:222
  81.6 2.2 %collective-permute-start.5 = (f32[128,256]{1,0:T(8,128)S(1)}, f32[128,256]{1,0:T(8,128)S(1)}, u32[]{:S(2)}, u32[]{:S(2)}) collective-permute-start(f32[128,256]{1,0:T(8,128)S(1)} %constant_dynamic-slice_fusion.3), channel_id=1, source_target_pairs={{0,4},{4,0},{8,12},{12,8},{16,20},{20,16},{24,28},{28,24},{32,36},... | collective-permute-start | bytes 393224 | tf_op jit(solution)/shard_map/ppermute | solution.py:234
  83.8 1.0 collective-permute-done.5
  84.8 0.1 collective-permute-start.6
  84.9 2.0 %collective-permute-start.7 = (f32[32,256]{1,0:T(8,128)S(1)}, f32[32,256]{1,0:T(8,128)S(1)}, u32[]{:S(2)}, u32[]{:S(2)}) collective-permute-start(f32[32,256]{1,0:T(8,128)S(1)} %get-tuple-element.33), channel_id=1, source_target_pairs={{0,16},{4,20},{8,24},{12,28},{16,0},{20,4},{24,8},{28,12},{32,48},... | collective-permute-start | bytes 98312 | tf_op jit(solution)/shard_map/ppermute | solution.py:234
  86.9 1.9 %collective-permute-start.8 = (f32[32,256]{1,0:T(8,128)S(1)}, f32[32,256]{1,0:T(8,128)S(1)}, u32[]{:S(2)}, u32[]{:S(2)}) collective-permute-start(f32[32,256]{1,0:T(8,128)S(1)} %get-tuple-element.34), channel_id=1, source_target_pairs={{0,24},{4,28},{8,16},{12,20},{16,8},{20,12},{24,0},{28,4},{32,56},... | collective-permute-start | bytes 98312 | tf_op jit(solution)/shard_map/ppermute | solution.py:234
  88.8 2.0 %collective-permute-done.7 = f32[32,256]{1,0:T(8,128)S(1)} collective-permute-done((f32[32,256]{1,0:T(8,128)S(1)}, f32[32,256]{1,0:T(8,128)S(1)}, u32[]{:S(2)}, u32[]{:S(2)}) %collective-permute-start.7) | collective-permute-done | bytes 32800 | tf_op jit(solution)/shard_map/ppermute | solution.py:234
  90.8 1.4 %collective-permute-done.8 = f32[32,256]{1,0:T(8,128)S(1)} collective-permute-done((f32[32,256]{1,0:T(8,128)S(1)}, f32[32,256]{1,0:T(8,128)S(1)}, u32[]{:S(2)}, u32[]{:S(2)}) %collective-permute-start.8) | collective-permute-done | bytes 32800 | tf_op jit(solution)/shard_map/ppermute | solution.py:234
  92.2 2.7 %collective-permute-start.10 = (f32[32,256]{1,0:T(8,128)S(1)}, f32[32,256]{1,0:T(8,128)S(1)}, u32[]{:S(2)}, u32[]{:S(2)}) collective-permute-start(f32[32,256]{1,0:T(8,128)S(1)} %add_add_fusion.1), channel_id=1, source_target_pairs={{0,2},{1,3},{2,0},{3,1},{4,6},{5,7},{6,4},{7,5},{8,10},{9,11},{10,... | collective-permute-start | bytes 98312 | tf_op jit(solution)/shard_map/ppermute | solution.py:234
  94.9 0.8 collective-permute-start.11
  95.6 1.5 %collective-permute-start.2 = (bf16[512,128]{1,0:T(8,128)(2,1)S(1)}, bf16[512,128]{1,0:T(8,128)(2,1)S(1)}, u32[]{:S(2)}, u32[]{:S(2)}) collective-permute-start(bf16[512,128]{1,0:T(8,128)(2,1)S(1)} %copy-done.8), channel_id=1, source_target_pairs={{0,1},{1,0},{2,3},{3,2},{4,5},{5,4},{6,7},{7,6},{8,9},{9,8},{10,11... | collective-permute-start | bytes 393224 | tf_op jit(solution)/shard_map/ppermute | solution.py:234
  97.1 1.7 %collective-permute-start.3 = (bf16[512,128]{1,0:T(8,128)(2,1)S(1)}, bf16[512,128]{1,0:T(8,128)(2,1)S(1)}, u32[]{:S(2)}, u32[]{:S(2)}) collective-permute-start(bf16[512,128]{1,0:T(8,128)(2,1)S(1)} %copy-done.7), channel_id=1, source_target_pairs={{0,2},{1,3},{2,0},{3,1},{4,6},{5,7},{6,4},{7,5},{8,10},{9,11},{10,... | collective-permute-start | bytes 393224 | tf_op jit(solution)/shard_map/ppermute | solution.py:234
  98.8 0.0 collective-permute-done.10
  98.8 0.8 collective-permute-start.4
  99.6 0.0 collective-permute-done.11
  99.6 2.0 %collective-permute-start.12 = (f32[32,256]{1,0:T(8,128)S(1)}, f32[32,256]{1,0:T(8,128)S(1)}, u32[]{:S(2)}, u32[]{:S(2)}) collective-permute-start(f32[32,256]{1,0:T(8,128)S(1)} %add_add_fusion), channel_id=1, source_target_pairs={{0,32},{4,36},{8,40},{12,44},{16,48},{20,52},{24,56},{28,60},{32,0... | collective-permute-start | bytes 98312 | tf_op jit(solution)/shard_map/ppermute | solution.py:234
  101.6 3.7 %collective-permute-done.12 = f32[32,256]{1,0:T(8,128)S(1)} collective-permute-done((f32[32,256]{1,0:T(8,128)S(1)}, f32[32,256]{1,0:T(8,128)S(1)}, u32[]{:S(2)}, u32[]{:S(2)}) %collective-permute-start.12) | collective-permute-done | bytes 32800 | tf_op jit(solution)/shard_map/ppermute | solution.py:234
  105.3 0.9 collective-permute-start.13
  106.2 2.9 %collective-permute-done.3.refs_2_ = bf16[512,128]{1,0:T(8,128)(2,1)S(1)} collective-permute-done((bf16[512,128]{1,0:T(8,128)(2,1)S(1)}, bf16[512,128]{1,0:T(8,128)(2,1)S(1)}, u32[]{:S(2)}, u32[]{:S(2)}) %collective-permute-start.3) | collective-permute-done | bytes 131104 | tf_op jit(solution)/shard_map/ppermute | solution.py:234
  109.1 1.9 %shard_map.106.start_ref = f32[512,256]{1,0:T(8,128)S(1)} custom-call(s32[32,128]{1,0:T(8,128)S(1)} %reshape.80.ids_ref, bf16[512,128]{1,0:T(8,128)(2,1)S(1)} %copy-done, bf16[512,128]{1,0:T(8,128)(2,1)S(1)} %collective-permute-done.2.refs_1_, bf16[512,128]{1,0:T(8,128)(2,1)S(1)} %collective-permute-done.3.refs_2_, ...), custom_call_target="tpu_custom_call" | custom-call | bytes 131072 | tf_op jit(solution)/shard_map/pallas_call | solution.py:327
  111.0 0.0 collective-permute-done.13
  111.1 1.4 %all-to-all-done.2 = bf16[256,16,128]{2,1,0:T(8,128)(2,1)S(1)} async-done(((bf16[256,16,128]{2,1,0:T(8,128)(2,1)}), bf16[256,16,128]{2,1,0:T(8,128)(2,1)S(1)}, u32[]{:S(2)}, u32[]{:S(2)}) %all-to-all-start.2) | async-done | bytes 1048608 | tf_op jit(solution)/shard_map/all_to_all | solution.py:222
  112.5 4.1 %collective-permute-start.14 = (f32[32,256]{1,0:T(8,128)S(1)}, f32[32,256]{1,0:T(8,128)S(1)}, u32[]{:S(2)}, u32[]{:S(2)}) collective-permute-start(f32[32,256]{1,0:T(8,128)S(1)} %add.62), channel_id=1, source_target_pairs={{0,128},{4,132},{8,136},{12,140},{16,144},{20,148},{24,152},{28,15... | collective-permute-start | bytes 98312 | tf_op jit(solution)/shard_map/ppermute | solution.py:234
  116.6 3.2 %shard_map.107.refs_0_ = bf16[512,256]{1,0:T(8,128)(2,1)S(1)} custom-call(s32[64,128]{1,0:T(8,128)S(1)} %reshape.82.ids_ref, bf16[4096,128]{1,0:T(8,128)(2,1)S(1)} %bitcast.22, f32[512,256]{1,0:T(8,128)S(1)} %shard_map.106.start_ref), custom_call_target="tpu_custom_call" | custom-call | flops 2147483648 | bytes 6291456 | tf_op jit(solution)/shard_map/pallas_call | solution.py:334
  119.8 0.4 collective-permute-start.17
  120.2 0.3 collective-permute-start.19
  120.5 2.3 %collective-permute-start.20 = (bf16[512,256]{1,0:T(8,128)(2,1)S(1)}, bf16[512,256]{1,0:T(8,128)(2,1)S(1)}, u32[]{:S(2)}, u32[]{:S(2)}) collective-permute-start(bf16[512,256]{1,0:T(8,128)(2,1)S(1)} %shard_map.107.refs_0_), channel_id=1, source_target_pairs={{0,2},{1,3},{2,0},{3,1},{4,6},{5,7},{6,4},{7,5},{8,10},{9,11},{10,... | collective-permute-start | bytes 786440 | tf_op jit(solution)/shard_map/ppermute | solution.py:226
  122.8 1.2 collective-permute-start.21
  124.0 1.7 %collective-permute-start.15 = (f32[32,256]{1,0:T(8,128)S(1)}, f32[32,256]{1,0:T(8,128)S(1)}, u32[]{:S(2)}, u32[]{:S(2)}) collective-permute-start(f32[32,256]{1,0:T(8,128)S(1)} %add.63), channel_id=1, source_target_pairs={{0,24},{4,28},{8,16},{12,20},{16,8},{20,12},{24,0},{28,4},{32,56},... | collective-permute-start | bytes 98312 | tf_op jit(solution)/shard_map/ppermute | solution.py:234
  125.7 1.4 %collective-permute-start.16 = (f32[32,256]{1,0:T(8,128)S(1)}, f32[32,256]{1,0:T(8,128)S(1)}, u32[]{:S(2)}, u32[]{:S(2)}) collective-permute-start(f32[32,256]{1,0:T(8,128)S(1)} %add.63), channel_id=1, source_target_pairs={{0,16},{4,20},{8,24},{12,28},{16,0},{20,4},{24,8},{28,12},{32,48},... | collective-permute-start | bytes 98312 | tf_op jit(solution)/shard_map/ppermute | solution.py:234
  127.1 1.1 collective-permute-done.15
  128.2 1.7 %collective-permute-done.16 = f32[32,256]{1,0:T(8,128)S(1)} collective-permute-done((f32[32,256]{1,0:T(8,128)S(1)}, f32[32,256]{1,0:T(8,128)S(1)}, u32[]{:S(2)}, u32[]{:S(2)}) %collective-permute-start.16) | collective-permute-done | bytes 32800 | tf_op jit(solution)/shard_map/ppermute | solution.py:234
  130.0 4.8 %collective-permute-start.18 = (f32[128,256]{1,0:T(8,128)S(1)}, f32[128,256]{1,0:T(8,128)S(1)}, u32[]{:S(2)}, u32[]{:S(2)}) collective-permute-start(f32[128,256]{1,0:T(8,128)S(1)} %maximum_select_fusion.1), channel_id=1, source_target_pairs={{0,4},{4,0},{8,12},{12,8},{16,20},{20,16},{24,28},{28,24},{32,36},... | collective-permute-start | bytes 393224 | tf_op jit(solution)/shard_map/ppermute | solution.py:234
  134.8 1.0 collective-permute-done.18
  135.8 0.7 fusion
  136.5 0.0 collective-permute-done.19.refs_1_
  136.5 1.7 %shard_map.108 = f32[2048,256]{1,0:T(8,128)} custom-call(bf16[512,256]{1,0:T(8,128)(2,1)S(1)} %shard_map.107.refs_0_, bf16[512,256]{1,0:T(8,128)(2,1)S(1)} %collective-permute-done.19.refs_1_, bf16[512,256]{1,0:T(8,128)(2,1)S(1)} %collective-permute-done.20.refs_2_, bf16[512,256]{1,0:T(8,128)(2,1)S(1)} %collective-permute-done.21.refs_3_), custom_call_target="tpu_custom_call" | custom-call | bytes 4194304 | tf_op jit(solution)/shard_map/pallas_call | solution.py:345
  (51 shorter events, 0.3 us)
Async XLA Ops:
  23.6 1.2 copy-start.2
  28.3 6.2 %copy-start.1 = (s32[1024]{0:T(1024)S(1)}, s32[1024]{0:T(1024)}, u32[]{:S(2)}) copy-start(s32[1024]{0:T(1024)} %param.9) | copy-start | bytes 12292
  28.3 7.6 %copy-start.3 = (bf16[2048,256]{1,0:T(8,128)(2,1)S(1)}, bf16[2048,256]{1,0:T(8,128)(2,1)}, u32[]{:S(2)}) copy-start(bf16[2048,256]{1,0:T(8,128)(2,1)} %table_ref.3) | copy-start | bytes 3145732
  28.3 33.1 %all-to-all-start.1 = ((bf16[64,32,256]{2,1,0:T(8,128)(2,1)}), bf16[64,32,256]{2,1,0:T(8,128)(2,1)S(1)}, u32[]{:S(2)}, u32[]{:S(2)}) async-start(bf16[64,32,256]{2,1,0:T(8,128)(2,1)} %bitcast.2), calls=%async_computation.1 | async-start | bytes 2097152 | tf_op jit(solution)/shard_map/all_to_all | solution.py:222
  34.5 2.9 %collective-permute-start = (s32[24,128]{1,0:T(8,128)S(1)}, s32[24,128]{1,0:T(8,128)S(1)}, u32[]{:S(2)}, u32[]{:S(2)}) collective-permute-start(s32[24,128]{1,0:T(8,128)S(1)} %add_bitcast_fusion.2), channel_id=1, source_target_pairs={{0,1},{1,0},{2,3},{3,2},{4,5},{5,4},{6,7},{7,6},{8,9},{9,8},{10,11... | collective-permute-start | bytes 36872 | tf_op jit(solution)/shard_map/ppermute | solution.py:234
  38.0 6.5 %collective-permute-start.1 = (s32[48,128]{1,0:T(8,128)S(1)}, s32[48,128]{1,0:T(8,128)S(1)}, u32[]{:S(2)}, u32[]{:S(2)}) collective-permute-start(s32[48,128]{1,0:T(8,128)S(1)} %add_bitcast_fusion), channel_id=1, source_target_pairs={{0,2},{1,3},{2,0},{3,1},{4,6},{5,7},{6,4},{7,5},{8,10},{9,11},{10,... | collective-permute-start | bytes 73736 | tf_op jit(solution)/shard_map/ppermute | solution.py:234
  61.3 1.0 copy-start.4
  72.4 9.2 %copy-start.5 = (f32[256,256]{1,0:T(8,128)S(1)}, f32[256,256]{1,0:T(8,128)}, u32[]{:S(2)}) copy-start(f32[256,256]{1,0:T(8,128)} %get-tuple-element.27) | copy-start | bytes 786436
  72.4 23.2 %copy-start.8 = (bf16[512,128]{1,0:T(8,128)(2,1)S(1)}, bf16[512,128]{1,0:T(8,128)(2,1)}, u32[]{:S(2)}) copy-start(bf16[512,128]{1,0:T(8,128)(2,1)} %get-tuple-element.24) | copy-start | bytes 393220
  72.4 24.7 %copy-start.7 = (bf16[512,128]{1,0:T(8,128)(2,1)S(1)}, bf16[512,128]{1,0:T(8,128)(2,1)}, u32[]{:S(2)}) copy-start(bf16[512,128]{1,0:T(8,128)(2,1)} %get-tuple-element.25) | copy-start | bytes 393220
  72.4 26.4 %copy-start.6 = (bf16[512,128]{1,0:T(8,128)(2,1)S(1)}, bf16[512,128]{1,0:T(8,128)(2,1)}, u32[]{:S(2)}) copy-start(bf16[512,128]{1,0:T(8,128)(2,1)} %get-tuple-element.26) | copy-start | bytes 393220
  72.4 36.7 %copy-start = (bf16[512,128]{1,0:T(8,128)(2,1)S(1)}, bf16[512,128]{1,0:T(8,128)(2,1)}, u32[]{:S(2)}) copy-start(bf16[512,128]{1,0:T(8,128)(2,1)} %get-tuple-element.23.refs_0_) | copy-start | bytes 393220
  72.4 40.1 %all-to-all-start.2 = ((bf16[256,16,128]{2,1,0:T(8,128)(2,1)}), bf16[256,16,128]{2,1,0:T(8,128)(2,1)S(1)}, u32[]{:S(2)}, u32[]{:S(2)}) async-start(bf16[256,16,128]{2,1,0:T(8,128)(2,1)} %get-tuple-element.21), calls=%async_computation.2 | async-start | bytes 2097152 | tf_op jit(solution)/shard_map/all_to_all | solution.py:222
  81.6 3.2 %collective-permute-start.5 = (f32[128,256]{1,0:T(8,128)S(1)}, f32[128,256]{1,0:T(8,128)S(1)}, u32[]{:S(2)}, u32[]{:S(2)}) collective-permute-start(f32[128,256]{1,0:T(8,128)S(1)} %constant_dynamic-slice_fusion.3), channel_id=1, source_target_pairs={{0,4},{4,0},{8,12},{12,8},{16,20},{20,16},{24,28},{28,24},{32,36},... | collective-permute-start | bytes 393224 | tf_op jit(solution)/shard_map/ppermute | solution.py:234
  84.8 3.9 %collective-permute-start.6 = (f32[32,256]{1,0:T(8,128)S(1)}, f32[32,256]{1,0:T(8,128)S(1)}, u32[]{:S(2)}, u32[]{:S(2)}) collective-permute-start(f32[32,256]{1,0:T(8,128)S(1)} %get-tuple-element.35), channel_id=1, source_target_pairs={{0,8},{4,12},{8,0},{12,4},{16,24},{20,28},{24,16},{28,20},{32,40},... | collective-permute-start | bytes 98312 | tf_op jit(solution)/shard_map/ppermute | solution.py:234
  84.9 5.8 %collective-permute-start.7 = (f32[32,256]{1,0:T(8,128)S(1)}, f32[32,256]{1,0:T(8,128)S(1)}, u32[]{:S(2)}, u32[]{:S(2)}) collective-permute-start(f32[32,256]{1,0:T(8,128)S(1)} %get-tuple-element.33), channel_id=1, source_target_pairs={{0,16},{4,20},{8,24},{12,28},{16,0},{20,4},{24,8},{28,12},{32,48},... | collective-permute-start | bytes 98312 | tf_op jit(solution)/shard_map/ppermute | solution.py:234
  86.9 5.3 %collective-permute-start.8 = (f32[32,256]{1,0:T(8,128)S(1)}, f32[32,256]{1,0:T(8,128)S(1)}, u32[]{:S(2)}, u32[]{:S(2)}) collective-permute-start(f32[32,256]{1,0:T(8,128)S(1)} %get-tuple-element.34), channel_id=1, source_target_pairs={{0,24},{4,28},{8,16},{12,20},{16,8},{20,12},{24,0},{28,4},{32,56},... | collective-permute-start | bytes 98312 | tf_op jit(solution)/shard_map/ppermute | solution.py:234
  92.2 6.6 %collective-permute-start.10 = (f32[32,256]{1,0:T(8,128)S(1)}, f32[32,256]{1,0:T(8,128)S(1)}, u32[]{:S(2)}, u32[]{:S(2)}) collective-permute-start(f32[32,256]{1,0:T(8,128)S(1)} %add_add_fusion.1), channel_id=1, source_target_pairs={{0,2},{1,3},{2,0},{3,1},{4,6},{5,7},{6,4},{7,5},{8,10},{9,11},{10,... | collective-permute-start | bytes 98312 | tf_op jit(solution)/shard_map/ppermute | solution.py:234
  94.9 4.7 %collective-permute-start.11 = (f32[32,256]{1,0:T(8,128)S(1)}, f32[32,256]{1,0:T(8,128)S(1)}, u32[]{:S(2)}, u32[]{:S(2)}) collective-permute-start(f32[32,256]{1,0:T(8,128)S(1)} %add_add_fusion.1), channel_id=1, source_target_pairs={{0,3},{1,2},{2,1},{3,0},{4,7},{5,6},{6,5},{7,4},{8,11},{9,10},{10,... | collective-permute-start | bytes 98312 | tf_op jit(solution)/shard_map/ppermute | solution.py:234
  95.6 4.0 %collective-permute-start.9 = (f32[32,256]{1,0:T(8,128)S(1)}, f32[32,256]{1,0:T(8,128)S(1)}, u32[]{:S(2)}, u32[]{:S(2)}) collective-permute-start(f32[32,256]{1,0:T(8,128)S(1)} %add_add_fusion.1), channel_id=1, source_target_pairs={{0,1},{1,0},{2,3},{3,2},{4,5},{5,4},{6,7},{7,6},{8,9},{9,8},{10,11... | collective-permute-start | bytes 98312 | tf_op jit(solution)/shard_map/ppermute | solution.py:234
  95.6 10.6 %collective-permute-start.2 = (bf16[512,128]{1,0:T(8,128)(2,1)S(1)}, bf16[512,128]{1,0:T(8,128)(2,1)S(1)}, u32[]{:S(2)}, u32[]{:S(2)}) collective-permute-start(bf16[512,128]{1,0:T(8,128)(2,1)S(1)} %copy-done.8), channel_id=1, source_target_pairs={{0,1},{1,0},{2,3},{3,2},{4,5},{5,4},{6,7},{7,6},{8,9},{9,8},{10,11... | collective-permute-start | bytes 393224 | tf_op jit(solution)/shard_map/ppermute | solution.py:234
  97.1 12.0 %collective-permute-start.3 = (bf16[512,128]{1,0:T(8,128)(2,1)S(1)}, bf16[512,128]{1,0:T(8,128)(2,1)S(1)}, u32[]{:S(2)}, u32[]{:S(2)}) collective-permute-start(bf16[512,128]{1,0:T(8,128)(2,1)S(1)} %copy-done.7), channel_id=1, source_target_pairs={{0,2},{1,3},{2,0},{3,1},{4,6},{5,7},{6,4},{7,5},{8,10},{9,11},{10,... | collective-permute-start | bytes 393224 | tf_op jit(solution)/shard_map/ppermute | solution.py:234
  98.8 10.3 %collective-permute-start.4 = (bf16[512,128]{1,0:T(8,128)(2,1)S(1)}, bf16[512,128]{1,0:T(8,128)(2,1)S(1)}, u32[]{:S(2)}, u32[]{:S(2)}) collective-permute-start(bf16[512,128]{1,0:T(8,128)(2,1)S(1)} %copy-done.6), channel_id=1, source_target_pairs={{0,3},{1,2},{2,1},{3,0},{4,7},{5,6},{6,5},{7,4},{8,11},{9,10},{10,... | collective-permute-start | bytes 393224 | tf_op jit(solution)/shard_map/ppermute | solution.py:234
  99.6 5.7 %collective-permute-start.12 = (f32[32,256]{1,0:T(8,128)S(1)}, f32[32,256]{1,0:T(8,128)S(1)}, u32[]{:S(2)}, u32[]{:S(2)}) collective-permute-start(f32[32,256]{1,0:T(8,128)S(1)} %add_add_fusion), channel_id=1, source_target_pairs={{0,32},{4,36},{8,40},{12,44},{16,48},{20,52},{24,56},{28,60},{32,0... | collective-permute-start | bytes 98312 | tf_op jit(solution)/shard_map/ppermute | solution.py:234
  105.3 5.8 %collective-permute-start.13 = (f32[32,256]{1,0:T(8,128)S(1)}, f32[32,256]{1,0:T(8,128)S(1)}, u32[]{:S(2)}, u32[]{:S(2)}) collective-permute-start(f32[32,256]{1,0:T(8,128)S(1)} %add.61), channel_id=1, source_target_pairs={{0,64},{4,68},{8,72},{12,76},{16,80},{20,84},{24,88},{28,92},{32,9... | collective-permute-start | bytes 98312 | tf_op jit(solution)/shard_map/ppermute | solution.py:234
  112.5 7.3 %collective-permute-start.14 = (f32[32,256]{1,0:T(8,128)S(1)}, f32[32,256]{1,0:T(8,128)S(1)}, u32[]{:S(2)}, u32[]{:S(2)}) collective-permute-start(f32[32,256]{1,0:T(8,128)S(1)} %add.62), channel_id=1, source_target_pairs={{0,128},{4,132},{8,136},{12,140},{16,144},{20,148},{24,152},{28,15... | collective-permute-start | bytes 98312 | tf_op jit(solution)/shard_map/ppermute | solution.py:234
  119.8 5.9 %collective-permute-start.17 = (f32[32,256]{1,0:T(8,128)S(1)}, f32[32,256]{1,0:T(8,128)S(1)}, u32[]{:S(2)}, u32[]{:S(2)}) collective-permute-start(f32[32,256]{1,0:T(8,128)S(1)} %add.63), channel_id=1, source_target_pairs={{0,8},{4,12},{8,0},{12,4},{16,24},{20,28},{24,16},{28,20},{32,40},... | collective-permute-start | bytes 98312 | tf_op jit(solution)/shard_map/ppermute | solution.py:234
  120.2 16.3 %collective-permute-start.19 = (bf16[512,256]{1,0:T(8,128)(2,1)S(1)}, bf16[512,256]{1,0:T(8,128)(2,1)S(1)}, u32[]{:S(2)}, u32[]{:S(2)}) collective-permute-start(bf16[512,256]{1,0:T(8,128)(2,1)S(1)} %shard_map.107.refs_0_), channel_id=1, source_target_pairs={{0,1},{1,2},{2,3},{3,0},{4,5},{5,6},{6,7},{7,4},{8,9},{9,10},{10,1... | collective-permute-start | bytes 786440 | tf_op jit(solution)/shard_map/ppermute | solution.py:226
  120.5 16.0 %collective-permute-start.20 = (bf16[512,256]{1,0:T(8,128)(2,1)S(1)}, bf16[512,256]{1,0:T(8,128)(2,1)S(1)}, u32[]{:S(2)}, u32[]{:S(2)}) collective-permute-start(bf16[512,256]{1,0:T(8,128)(2,1)S(1)} %shard_map.107.refs_0_), channel_id=1, source_target_pairs={{0,2},{1,3},{2,0},{3,1},{4,6},{5,7},{6,4},{7,5},{8,10},{9,11},{10,... | collective-permute-start | bytes 786440 | tf_op jit(solution)/shard_map/ppermute | solution.py:226
  122.8 13.7 %collective-permute-start.21 = (bf16[512,256]{1,0:T(8,128)(2,1)S(1)}, bf16[512,256]{1,0:T(8,128)(2,1)S(1)}, u32[]{:S(2)}, u32[]{:S(2)}) collective-permute-start(bf16[512,256]{1,0:T(8,128)(2,1)S(1)} %shard_map.107.refs_0_), channel_id=1, source_target_pairs={{0,3},{1,0},{2,1},{3,2},{4,7},{5,4},{6,5},{7,6},{8,11},{9,8},{10,9... | collective-permute-start | bytes 786440 | tf_op jit(solution)/shard_map/ppermute | solution.py:226
  124.0 4.3 %collective-permute-start.15 = (f32[32,256]{1,0:T(8,128)S(1)}, f32[32,256]{1,0:T(8,128)S(1)}, u32[]{:S(2)}, u32[]{:S(2)}) collective-permute-start(f32[32,256]{1,0:T(8,128)S(1)} %add.63), channel_id=1, source_target_pairs={{0,24},{4,28},{8,16},{12,20},{16,8},{20,12},{24,0},{28,4},{32,56},... | collective-permute-start | bytes 98312 | tf_op jit(solution)/shard_map/ppermute | solution.py:234
  125.7 4.3 %collective-permute-start.16 = (f32[32,256]{1,0:T(8,128)S(1)}, f32[32,256]{1,0:T(8,128)S(1)}, u32[]{:S(2)}, u32[]{:S(2)}) collective-permute-start(f32[32,256]{1,0:T(8,128)S(1)} %add.63), channel_id=1, source_target_pairs={{0,16},{4,20},{8,24},{12,28},{16,0},{20,4},{24,8},{28,12},{32,48},... | collective-permute-start | bytes 98312 | tf_op jit(solution)/shard_map/ppermute | solution.py:234
  130.0 5.8 %collective-permute-start.18 = (f32[128,256]{1,0:T(8,128)S(1)}, f32[128,256]{1,0:T(8,128)S(1)}, u32[]{:S(2)}, u32[]{:S(2)}) collective-permute-start(f32[128,256]{1,0:T(8,128)S(1)} %maximum_select_fusion.1), channel_id=1, source_target_pairs={{0,4},{4,0},{8,12},{12,8},{16,20},{20,16},{24,28},{28,24},{32,36},... | collective-permute-start | bytes 393224 | tf_op jit(solution)/shard_map/ppermute | solution.py:234

commit v2 on v1

--- a/solution.py
+++ b/solution.py
@@ -318,7 +318,7 @@
             pltpu.SemaphoreType.DMA((5 + batch_rows // 256,)),
             pltpu.SemaphoreType.DMA((2 + replicas + owners // 8,)),
         ],
-        compiler_params=pltpu.CompilerParams(vmem_limit_bytes=56 * 2**20),
+        compiler_params=pltpu.CompilerParams(vmem_limit_bytes=50 * 2**20),
         cost_estimate=pl.CostEstimate(flops=2 * 7 * 2**20 * width, bytes_accessed=10 * 2**20, transcendentals=0),
     )(halo_counts, halo_rows, adj_halo, local, weight, cotangent, adj_local)
     arrived = exchange(messages, both).reshape(owners * replicas * slots // 2, 128)

time: 139 us -> 136 us (0.978)
  Pallas kernels: 21.7 us -> 20.2 us
    pallas_call x1, Pallas kernels: 10.1 us -> 8.62 us  [body(): pl.pallas_call(middle_kernel, out_shape=(like((batch_rows, width), BF16),...]
    unnamed x20 -> x14, local copies, waits for them, and re-layouts: 3.03 us -> 2.05 us
where the time goes in v2:
time: 136 us
  starting transfers between devices  51.3 us (38%)
  waiting for transfers between devices  32.4 us (24%)
  blocking collectives  22.2 us (16%)
  Pallas kernels  20.2 us (15%)
  local copies, waits for them, and re-layouts  3.94 us (3%)
  matrix products  3.29 us (2%)
  other arithmetic  1.59 us (1%)
    ppermute x19, starting transfers between devices, swap(): lax.ppermute(x, axis, [(i, i ^ bit) for i in range(lax.axis_size(axis))])  33.5 us
    all_to_all x1, blocking collectives, exchange(): return lax.all_to_all(x, axes, split_axis=0, concat_axis=0, tiled=True)  22.2 us
    all_to_all x2, waiting for transfers between devices, exchange(): return lax.all_to_all(x, axes, split_axis=0, concat_axis=0, tiled=True)  17.5 us
    ppermute x19, waiting for transfers between devices, swap(): lax.ppermute(x, axis, [(i, i ^ bit) for i in range(lax.axis_size(axis))])  14.8 us
    all_to_all x2, starting transfers between devices, exchange(): return lax.all_to_all(x, axes, split_axis=0, concat_axis=0, tiled=True)  14 us
    pallas_call x1, Pallas kernels, body(): pl.pallas_call(middle_kernel, out_shape=(like((batch_rows, width), BF16),...  8.62 us
    pallas_call x2, Pallas kernels, gather_rows(): vmem_call(gather_kernel, jax.ShapeDtypeStruct((count, width), BF16), [VME...  4.85 us
    ppermute x3, starting transfers between devices, from_behind(): return lax.ppermute(x, 'rep', [(i, (i + by) % 4) for i in range(4)])  3.74 us
  transfers between devices with their start and end apart: 24, of which 11 were waited for; matrix products, arithmetic and copies ran while one was open for 5% of the time, Pallas kernels for 5%

profile of v2, /device:TPU:1, one launch (start us, length us, event | category | flops | bytes accessed | tf_op | source)
XLA Modules:
  0.0 135.8 jit_solution(12956012118732640133)
XLA Ops:
  0.6 0.8 copy.22
  1.4 22.2 %all_to_all.15 = s32[64,1,32]{2,1,0:T(1,128)S(1)} all-to-all(s32[64,1,32]{2,1,0:T(1,128)S(1)} %bitcast.26), channel_id=1, replica_groups=mesh['dom'=64,'rep'=4] {'dom'}, dimensions={0} | all-to-all | bytes 16384 | tf_op jit(solution)/shard_map/all_to_all | solution.py:222
  23.6 1.2 copy-done.1
  24.8 3.5 %shard_map.103 = bf16[2048,256]{1,0:T(8,128)(2,1)} custom-call(s32[64,32]{1,0:T(8,128)S(1)} %bitcast.24, bf16[2048,256]{1,0:T(8,128)(2,1)S(1)} %copy-done.1), custom_call_target="tpu_custom_call" | custom-call | flops 2147483648 | bytes 2097152 | tf_op jit(solution)/shard_map/pallas_call | solution.py:46
  28.3 4.9 %all-to-all-start.1 = ((bf16[64,32,256]{2,1,0:T(8,128)(2,1)}), bf16[64,32,256]{2,1,0:T(8,128)(2,1)S(1)}, u32[]{:S(2)}, u32[]{:S(2)}) async-start(bf16[64,32,256]{2,1,0:T(8,128)(2,1)} %bitcast.2), calls=%async_computation.1 | async-start | bytes 2097152 | tf_op jit(solution)/shard_map/all_to_all | solution.py:222
  33.2 0.5 broadcast.7
  33.7 0.7 reduce.3
  34.4 0.1 reshape_reshape_reshape.3
  34.5 1.4 %collective-permute-start = (s32[24,128]{1,0:T(8,128)S(1)}, s32[24,128]{1,0:T(8,128)S(1)}, u32[]{:S(2)}, u32[]{:S(2)}) collective-permute-start(s32[24,128]{1,0:T(8,128)S(1)} %add_bitcast_fusion.2), channel_id=1, source_target_pairs={{0,1},{1,0},{2,3},{3,2},{4,5},{5,4},{6,7},{7,6},{8,9},{9,8},{10,11... | collective-permute-start | bytes 36872 | tf_op jit(solution)/shard_map/ppermute | solution.py:234
  35.9 1.4 %shard_map.104 = bf16[1024,256]{1,0:T(8,128)(2,1)S(1)} custom-call(s32[8,128]{1,0:T(8,128)S(1)} %bitcast.25, bf16[2048,256]{1,0:T(8,128)(2,1)S(1)} %copy-done.2), custom_call_target="tpu_custom_call" | custom-call | flops 1073741824 | bytes 1048576 | tf_op jit(solution)/shard_map/pallas_call | solution.py:46
  37.3 0.1 copy.23
  37.4 0.1 collective-permute-done
  37.4 0.1 reshape.77
  37.6 0.1 copy.24
  37.6 0.1 copy.26
  37.8 0.2 select_n.68
  38.0 0.0 copy-start.3
  38.0 0.0 copy-start.4
  38.0 0.0 copy-start.5
  38.0 3.2 %collective-permute-start.1 = (s32[48,128]{1,0:T(8,128)S(1)}, s32[48,128]{1,0:T(8,128)S(1)}, u32[]{:S(2)}, u32[]{:S(2)}) collective-permute-start(s32[48,128]{1,0:T(8,128)S(1)} %add_bitcast_fusion), channel_id=1, source_target_pairs={{0,2},{1,3},{2,0},{3,1},{4,6},{5,7},{6,4},{7,5},{8,10},{9,11},{10,... | collective-permute-start | bytes 73736 | tf_op jit(solution)/shard_map/ppermute | solution.py:234
  41.2 3.3 %convolution_bitcast_fusion.local_hbm = f32[1024,256]{1,0:T(8,128)} fusion(bf16[1024,1024]{1,0:T(8,128)(2,1)} %adj_local_hbm.1, bf16[1024,256]{1,0:T(8,128)(2,1)S(1)} %shard_map.104), kind=kOutput, calls=%fused_computation | convolution fusion | flops 536870912 | bytes 3670016 | tf_op jit(solution)/shard_map/dot_general | solution.py:294
  44.5 0.0 collective-permute-done.1
  44.5 0.2 reshape.81
  44.7 0.1 copy.28
  44.8 0.1 copy.30
  45.0 0.2 reshape.82.ids_ref
  45.3 16.1 %all-to-all-done.1 = bf16[64,32,256]{2,1,0:T(8,128)(2,1)S(1)} async-done(((bf16[64,32,256]{2,1,0:T(8,128)(2,1)}), bf16[64,32,256]{2,1,0:T(8,128)(2,1)S(1)}, u32[]{:S(2)}, u32[]{:S(2)}) %all-to-all-start.1) | async-done | bytes 1048608 | tf_op jit(solution)/shard_map/all_to_all | solution.py:222
  61.3 8.6 %shard_map.105 = (bf16[1024,256]{1,0:T(8,128)(2,1)}, f32[256,256]{1,0:T(8,128)S(1)}, bf16[256,16,128]{2,1,0:T(8,128)(2,1)}, bf16[512,128]{1,0:T(8,128)(2,1)S(1)}...) custom-call(s32[1,64]{1,0:T(1,128)S(1)} %copy-done.5, ...), custom_call_target="tpu_custom_call" | custom-call | flops 3758096384 | bytes 10485760 | tf_op jit(solution)/shard_map/pallas_call | solution.py:296
  70.0 9.1 %all-to-all-start.2 = ((bf16[256,16,128]{2,1,0:T(8,128)(2,1)}), bf16[256,16,128]{2,1,0:T(8,128)(2,1)S(1)}, u32[]{:S(2)}, u32[]{:S(2)}) async-start(bf16[256,16,128]{2,1,0:T(8,128)(2,1)} %get-tuple-element.21), calls=%async_computation.2 | async-start | bytes 2097152 | tf_op jit(solution)/shard_map/all_to_all | solution.py:222
  79.1 2.2 %collective-permute-start.5 = (f32[128,256]{1,0:T(8,128)S(1)}, f32[128,256]{1,0:T(8,128)S(1)}, u32[]{:S(2)}, u32[]{:S(2)}) collective-permute-start(f32[128,256]{1,0:T(8,128)S(1)} %constant_dynamic-slice_fusion.3), channel_id=1, source_target_pairs={{0,4},{4,0},{8,12},{12,8},{16,20},{20,16},{24,28},{28,24},{32,36},... | collective-permute-start | bytes 393224 | tf_op jit(solution)/shard_map/ppermute | solution.py:234
  81.3 1.0 collective-permute-done.5
  82.4 0.1 collective-permute-start.6
  82.5 2.0 %collective-permute-start.7 = (f32[32,256]{1,0:T(8,128)S(1)}, f32[32,256]{1,0:T(8,128)S(1)}, u32[]{:S(2)}, u32[]{:S(2)}) collective-permute-start(f32[32,256]{1,0:T(8,128)S(1)} %get-tuple-element.33), channel_id=1, source_target_pairs={{0,16},{4,20},{8,24},{12,28},{16,0},{20,4},{24,8},{28,12},{32,48},... | collective-permute-start | bytes 98312 | tf_op jit(solution)/shard_map/ppermute | solution.py:234
  84.5 1.9 %collective-permute-start.8 = (f32[32,256]{1,0:T(8,128)S(1)}, f32[32,256]{1,0:T(8,128)S(1)}, u32[]{:S(2)}, u32[]{:S(2)}) collective-permute-start(f32[32,256]{1,0:T(8,128)S(1)} %get-tuple-element.34), channel_id=1, source_target_pairs={{0,24},{4,28},{8,16},{12,20},{16,8},{20,12},{24,0},{28,4},{32,56},... | collective-permute-start | bytes 98312 | tf_op jit(solution)/shard_map/ppermute | solution.py:234
  86.3 0.0 collective-permute-done.6
  86.3 2.0 %collective-permute-done.7 = f32[32,256]{1,0:T(8,128)S(1)} collective-permute-done((f32[32,256]{1,0:T(8,128)S(1)}, f32[32,256]{1,0:T(8,128)S(1)}, u32[]{:S(2)}, u32[]{:S(2)}) %collective-permute-start.7) | collective-permute-done | bytes 32800 | tf_op jit(solution)/shard_map/ppermute | solution.py:234
  88.3 1.4 %collective-permute-done.8 = f32[32,256]{1,0:T(8,128)S(1)} collective-permute-done((f32[32,256]{1,0:T(8,128)S(1)}, f32[32,256]{1,0:T(8,128)S(1)}, u32[]{:S(2)}, u32[]{:S(2)}) %collective-permute-start.8) | collective-permute-done | bytes 32800 | tf_op jit(solution)/shard_map/ppermute | solution.py:234
  89.7 2.7 %collective-permute-start.10 = (f32[32,256]{1,0:T(8,128)S(1)}, f32[32,256]{1,0:T(8,128)S(1)}, u32[]{:S(2)}, u32[]{:S(2)}) collective-permute-start(f32[32,256]{1,0:T(8,128)S(1)} %add_add_fusion.1), channel_id=1, source_target_pairs={{0,2},{1,3},{2,0},{3,1},{4,6},{5,7},{6,4},{7,5},{8,10},{9,11},{10,... | collective-permute-start | bytes 98312 | tf_op jit(solution)/shard_map/ppermute | solution.py:234
  92.4 0.7 collective-permute-start.11
  93.1 0.0 collective-permute-start.9
  93.1 1.5 %collective-permute-start.2 = (bf16[512,128]{1,0:T(8,128)(2,1)S(1)}, bf16[512,128]{1,0:T(8,128)(2,1)S(1)}, u32[]{:S(2)}, u32[]{:S(2)}) collective-permute-start(bf16[512,128]{1,0:T(8,128)(2,1)S(1)} %get-tuple-element.24), channel_id=1, source_target_pairs={{0,1},{1,0},{2,3},{3,2},{4,5},{5,4},{6,7},{7,6},{8,9},{9,8},{10,11... | collective-permute-start | bytes 393224 | tf_op jit(solution)/shard_map/ppermute | solution.py:234
  94.6 1.7 %collective-permute-start.3 = (bf16[512,128]{1,0:T(8,128)(2,1)S(1)}, bf16[512,128]{1,0:T(8,128)(2,1)S(1)}, u32[]{:S(2)}, u32[]{:S(2)}) collective-permute-start(bf16[512,128]{1,0:T(8,128)(2,1)S(1)} %get-tuple-element.25), channel_id=1, source_target_pairs={{0,2},{1,3},{2,0},{3,1},{4,6},{5,7},{6,4},{7,5},{8,10},{9,11},{10,... | collective-permute-start | bytes 393224 | tf_op jit(solution)/shard_map/ppermute | solution.py:234
  96.3 0.7 collective-permute-start.4
  97.1 2.1 %collective-permute-start.12 = (f32[32,256]{1,0:T(8,128)S(1)}, f32[32,256]{1,0:T(8,128)S(1)}, u32[]{:S(2)}, u32[]{:S(2)}) collective-permute-start(f32[32,256]{1,0:T(8,128)S(1)} %add_add_fusion), channel_id=1, source_target_pairs={{0,32},{4,36},{8,40},{12,44},{16,48},{20,52},{24,56},{28,60},{32,0... | collective-permute-start | bytes 98312 | tf_op jit(solution)/shard_map/ppermute | solution.py:234
  99.1 3.7 %collective-permute-done.12 = f32[32,256]{1,0:T(8,128)S(1)} collective-permute-done((f32[32,256]{1,0:T(8,128)S(1)}, f32[32,256]{1,0:T(8,128)S(1)}, u32[]{:S(2)}, u32[]{:S(2)}) %collective-permute-start.12) | collective-permute-done | bytes 32800 | tf_op jit(solution)/shard_map/ppermute | solution.py:234
  102.8 0.9 collective-permute-start.13
  103.7 2.9 %collective-permute-done.3.refs_2_ = bf16[512,128]{1,0:T(8,128)(2,1)S(1)} collective-permute-done((bf16[512,128]{1,0:T(8,128)(2,1)S(1)}, bf16[512,128]{1,0:T(8,128)(2,1)S(1)}, u32[]{:S(2)}, u32[]{:S(2)}) %collective-permute-start.3) | collective-permute-done | bytes 131104 | tf_op jit(solution)/shard_map/ppermute | solution.py:234
  106.6 0.0 collective-permute-done.4.refs_3_
  106.6 1.9 %shard_map.106.start_ref = f32[512,256]{1,0:T(8,128)S(1)} custom-call(s32[32,128]{1,0:T(8,128)S(1)} %reshape.80.ids_ref, bf16[512,128]{1,0:T(8,128)(2,1)S(1)} %get-tuple-element.23.refs_0_, bf16[512,128]{1,0:T(8,128)(2,1)S(1)} %collective-permute-done.2.refs_1_, bf16[512,128]{1,0:T(8,128)(2,1)S(1)} %collective-permute-done.3.refs_2_, ...), custom_call_target="tpu_custom_call" | custom-call | bytes 131072 | tf_op jit(solution)/shard_map/pallas_call | solution.py:327
  108.6 1.4 %all-to-all-done.2 = bf16[256,16,128]{2,1,0:T(8,128)(2,1)S(1)} async-done(((bf16[256,16,128]{2,1,0:T(8,128)(2,1)}), bf16[256,16,128]{2,1,0:T(8,128)(2,1)S(1)}, u32[]{:S(2)}, u32[]{:S(2)}) %all-to-all-start.2) | async-done | bytes 1048608 | tf_op jit(solution)/shard_map/all_to_all | solution.py:222
  110.0 4.1 %collective-permute-start.14 = (f32[32,256]{1,0:T(8,128)S(1)}, f32[32,256]{1,0:T(8,128)S(1)}, u32[]{:S(2)}, u32[]{:S(2)}) collective-permute-start(f32[32,256]{1,0:T(8,128)S(1)} %add.62), channel_id=1, source_target_pairs={{0,128},{4,132},{8,136},{12,140},{16,144},{20,148},{24,152},{28,15... | collective-permute-start | bytes 98312 | tf_op jit(solution)/shard_map/ppermute | solution.py:234
  114.1 3.2 %shard_map.107.refs_0_ = bf16[512,256]{1,0:T(8,128)(2,1)S(1)} custom-call(s32[64,128]{1,0:T(8,128)S(1)} %reshape.82.ids_ref, bf16[4096,128]{1,0:T(8,128)(2,1)S(1)} %bitcast.22, f32[512,256]{1,0:T(8,128)S(1)} %shard_map.106.start_ref), custom_call_target="tpu_custom_call" | custom-call | flops 2147483648 | bytes 6291456 | tf_op jit(solution)/shard_map/pallas_call | solution.py:334
  117.4 0.4 collective-permute-start.17
  117.8 0.3 collective-permute-start.19
  118.1 2.3 %collective-permute-start.20 = (bf16[512,256]{1,0:T(8,128)(2,1)S(1)}, bf16[512,256]{1,0:T(8,128)(2,1)S(1)}, u32[]{:S(2)}, u32[]{:S(2)}) collective-permute-start(bf16[512,256]{1,0:T(8,128)(2,1)S(1)} %shard_map.107.refs_0_), channel_id=1, source_target_pairs={{0,2},{1,3},{2,0},{3,1},{4,6},{5,7},{6,4},{7,5},{8,10},{9,11},{10,... | collective-permute-start | bytes 786440 | tf_op jit(solution)/shard_map/ppermute | solution.py:226
  120.3 1.2 collective-permute-start.21
  121.5 1.7 %collective-permute-start.15 = (f32[32,256]{1,0:T(8,128)S(1)}, f32[32,256]{1,0:T(8,128)S(1)}, u32[]{:S(2)}, u32[]{:S(2)}) collective-permute-start(f32[32,256]{1,0:T(8,128)S(1)} %add.63), channel_id=1, source_target_pairs={{0,24},{4,28},{8,16},{12,20},{16,8},{20,12},{24,0},{28,4},{32,56},... | collective-permute-start | bytes 98312 | tf_op jit(solution)/shard_map/ppermute | solution.py:234
  123.3 1.4 %collective-permute-start.16 = (f32[32,256]{1,0:T(8,128)S(1)}, f32[32,256]{1,0:T(8,128)S(1)}, u32[]{:S(2)}, u32[]{:S(2)}) collective-permute-start(f32[32,256]{1,0:T(8,128)S(1)} %add.63), channel_id=1, source_target_pairs={{0,16},{4,20},{8,24},{12,28},{16,0},{20,4},{24,8},{28,12},{32,48},... | collective-permute-start | bytes 98312 | tf_op jit(solution)/shard_map/ppermute | solution.py:234
  124.7 1.1 collective-permute-done.15
  125.8 1.7 %collective-permute-done.16 = f32[32,256]{1,0:T(8,128)S(1)} collective-permute-done((f32[32,256]{1,0:T(8,128)S(1)}, f32[32,256]{1,0:T(8,128)S(1)}, u32[]{:S(2)}, u32[]{:S(2)}) %collective-permute-start.16) | collective-permute-done | bytes 32800 | tf_op jit(solution)/shard_map/ppermute | solution.py:234
  127.6 4.8 %collective-permute-start.18 = (f32[128,256]{1,0:T(8,128)S(1)}, f32[128,256]{1,0:T(8,128)S(1)}, u32[]{:S(2)}, u32[]{:S(2)}) collective-permute-start(f32[128,256]{1,0:T(8,128)S(1)} %maximum_select_fusion.1), channel_id=1, source_target_pairs={{0,4},{4,0},{8,12},{12,8},{16,20},{20,16},{24,28},{28,24},{32,36},... | collective-permute-start | bytes 393224 | tf_op jit(solution)/shard_map/ppermute | solution.py:234
  132.3 1.0 collective-permute-done.18
  133.3 0.7 fusion
  134.1 1.7 %shard_map.108 = f32[2048,256]{1,0:T(8,128)} custom-call(bf16[512,256]{1,0:T(8,128)(2,1)S(1)} %shard_map.107.refs_0_, bf16[512,256]{1,0:T(8,128)(2,1)S(1)} %collective-permute-done.19.refs_1_, bf16[512,256]{1,0:T(8,128)(2,1)S(1)} %collective-permute-done.20.refs_2_, bf16[512,256]{1,0:T(8,128)(2,1)S(1)} %collective-permute-done.21.refs_3_), custom_call_target="tpu_custom_call" | custom-call | bytes 4194304 | tf_op jit(solution)/shard_map/pallas_call | solution.py:345
  (45 shorter events, 0.3 us)
Async XLA Ops:
  23.6 1.2 copy-start.1
  28.3 6.2 %copy-start = (s32[1024]{0:T(1024)S(1)}, s32[1024]{0:T(1024)}, u32[]{:S(2)}) copy-start(s32[1024]{0:T(1024)} %param.9) | copy-start | bytes 12292
  28.3 7.6 %copy-start.2 = (bf16[2048,256]{1,0:T(8,128)(2,1)S(1)}, bf16[2048,256]{1,0:T(8,128)(2,1)}, u32[]{:S(2)}) copy-start(bf16[2048,256]{1,0:T(8,128)(2,1)} %table_ref.3) | copy-start | bytes 3145732
  28.3 33.1 %all-to-all-start.1 = ((bf16[64,32,256]{2,1,0:T(8,128)(2,1)}), bf16[64,32,256]{2,1,0:T(8,128)(2,1)S(1)}, u32[]{:S(2)}, u32[]{:S(2)}) async-start(bf16[64,32,256]{2,1,0:T(8,128)(2,1)} %bitcast.2), calls=%async_computation.1 | async-start | bytes 2097152 | tf_op jit(solution)/shard_map/all_to_all | solution.py:222
  34.5 2.9 %collective-permute-start = (s32[24,128]{1,0:T(8,128)S(1)}, s32[24,128]{1,0:T(8,128)S(1)}, u32[]{:S(2)}, u32[]{:S(2)}) collective-permute-start(s32[24,128]{1,0:T(8,128)S(1)} %add_bitcast_fusion.2), channel_id=1, source_target_pairs={{0,1},{1,0},{2,3},{3,2},{4,5},{5,4},{6,7},{7,6},{8,9},{9,8},{10,11... | collective-permute-start | bytes 36872 | tf_op jit(solution)/shard_map/ppermute | solution.py:234
  38.0 23.3 %copy-start.3 = (bf16[1024,256]{1,0:T(8,128)(2,1)S(1)}, bf16[1024,256]{1,0:T(8,128)(2,1)}, u32[]{:S(2)}) copy-start(bf16[1024,256]{1,0:T(8,128)(2,1)} %cotangent_hbm.1) | copy-start | bytes 1572868
  38.0 23.3 %copy-start.4 = (bf16[256,256]{1,0:T(8,128)(2,1)S(1)}, bf16[256,256]{1,0:T(8,128)(2,1)}, u32[]{:S(2)}) copy-start(bf16[256,256]{1,0:T(8,128)(2,1)} %weight_hbm.1) | copy-start | bytes 393220
  38.0 23.3 %copy-start.5 = (s32[1,64]{1,0:T(1,128)S(1)}, s32[1,64]{1,0:T(1,128)}, u32[]{:S(2)}) copy-start(s32[1,64]{1,0:T(1,128)} %counts_hbm.1) | copy-start | bytes 772
  38.0 6.5 %collective-permute-start.1 = (s32[48,128]{1,0:T(8,128)S(1)}, s32[48,128]{1,0:T(8,128)S(1)}, u32[]{:S(2)}, u32[]{:S(2)}) collective-permute-start(s32[48,128]{1,0:T(8,128)S(1)} %add_bitcast_fusion), channel_id=1, source_target_pairs={{0,2},{1,3},{2,0},{3,1},{4,6},{5,7},{6,4},{7,5},{8,10},{9,11},{10,... | collective-permute-start | bytes 73736 | tf_op jit(solution)/shard_map/ppermute | solution.py:234
  70.0 40.1 %all-to-all-start.2 = ((bf16[256,16,128]{2,1,0:T(8,128)(2,1)}), bf16[256,16,128]{2,1,0:T(8,128)(2,1)S(1)}, u32[]{:S(2)}, u32[]{:S(2)}) async-start(bf16[256,16,128]{2,1,0:T(8,128)(2,1)} %get-tuple-element.21), calls=%async_computation.2 | async-start | bytes 2097152 | tf_op jit(solution)/shard_map/all_to_all | solution.py:222
  79.1 3.2 %collective-permute-start.5 = (f32[128,256]{1,0:T(8,128)S(1)}, f32[128,256]{1,0:T(8,128)S(1)}, u32[]{:S(2)}, u32[]{:S(2)}) collective-permute-start(f32[128,256]{1,0:T(8,128)S(1)} %constant_dynamic-slice_fusion.3), channel_id=1, source_target_pairs={{0,4},{4,0},{8,12},{12,8},{16,20},{20,16},{24,28},{28,24},{32,36},... | collective-permute-start | bytes 393224 | tf_op jit(solution)/shard_map/ppermute | solution.py:234
  82.4 3.9 %collective-permute-start.6 = (f32[32,256]{1,0:T(8,128)S(1)}, f32[32,256]{1,0:T(8,128)S(1)}, u32[]{:S(2)}, u32[]{:S(2)}) collective-permute-start(f32[32,256]{1,0:T(8,128)S(1)} %get-tuple-element.35), channel_id=1, source_target_pairs={{0,8},{4,12},{8,0},{12,4},{16,24},{20,28},{24,16},{28,20},{32,40},... | collective-permute-start | bytes 98312 | tf_op jit(solution)/shard_map/ppermute | solution.py:234
  82.5 5.8 %collective-permute-start.7 = (f32[32,256]{1,0:T(8,128)S(1)}, f32[32,256]{1,0:T(8,128)S(1)}, u32[]{:S(2)}, u32[]{:S(2)}) collective-permute-start(f32[32,256]{1,0:T(8,128)S(1)} %get-tuple-element.33), channel_id=1, source_target_pairs={{0,16},{4,20},{8,24},{12,28},{16,0},{20,4},{24,8},{28,12},{32,48},... | collective-permute-start | bytes 98312 | tf_op jit(solution)/shard_map/ppermute | solution.py:234
  84.5 5.3 %collective-permute-start.8 = (f32[32,256]{1,0:T(8,128)S(1)}, f32[32,256]{1,0:T(8,128)S(1)}, u32[]{:S(2)}, u32[]{:S(2)}) collective-permute-start(f32[32,256]{1,0:T(8,128)S(1)} %get-tuple-element.34), channel_id=1, source_target_pairs={{0,24},{4,28},{8,16},{12,20},{16,8},{20,12},{24,0},{28,4},{32,56},... | collective-permute-start | bytes 98312 | tf_op jit(solution)/shard_map/ppermute | solution.py:234
  89.7 6.5 %collective-permute-start.10 = (f32[32,256]{1,0:T(8,128)S(1)}, f32[32,256]{1,0:T(8,128)S(1)}, u32[]{:S(2)}, u32[]{:S(2)}) collective-permute-start(f32[32,256]{1,0:T(8,128)S(1)} %add_add_fusion.1), channel_id=1, source_target_pairs={{0,2},{1,3},{2,0},{3,1},{4,6},{5,7},{6,4},{7,5},{8,10},{9,11},{10,... | collective-permute-start | bytes 98312 | tf_op jit(solution)/shard_map/ppermute | solution.py:234
  92.4 4.6 %collective-permute-start.11 = (f32[32,256]{1,0:T(8,128)S(1)}, f32[32,256]{1,0:T(8,128)S(1)}, u32[]{:S(2)}, u32[]{:S(2)}) collective-permute-start(f32[32,256]{1,0:T(8,128)S(1)} %add_add_fusion.1), channel_id=1, source_target_pairs={{0,3},{1,2},{2,1},{3,0},{4,7},{5,6},{6,5},{7,4},{8,11},{9,10},{10,... | collective-permute-start | bytes 98312 | tf_op jit(solution)/shard_map/ppermute | solution.py:234
  93.1 3.9 %collective-permute-start.9 = (f32[32,256]{1,0:T(8,128)S(1)}, f32[32,256]{1,0:T(8,128)S(1)}, u32[]{:S(2)}, u32[]{:S(2)}) collective-permute-start(f32[32,256]{1,0:T(8,128)S(1)} %add_add_fusion.1), channel_id=1, source_target_pairs={{0,1},{1,0},{2,3},{3,2},{4,5},{5,4},{6,7},{7,6},{8,9},{9,8},{10,11... | collective-permute-start | bytes 98312 | tf_op jit(solution)/shard_map/ppermute | solution.py:234
  93.1 10.6 %collective-permute-start.2 = (bf16[512,128]{1,0:T(8,128)(2,1)S(1)}, bf16[512,128]{1,0:T(8,128)(2,1)S(1)}, u32[]{:S(2)}, u32[]{:S(2)}) collective-permute-start(bf16[512,128]{1,0:T(8,128)(2,1)S(1)} %get-tuple-element.24), channel_id=1, source_target_pairs={{0,1},{1,0},{2,3},{3,2},{4,5},{5,4},{6,7},{7,6},{8,9},{9,8},{10,11... | collective-permute-start | bytes 393224 | tf_op jit(solution)/shard_map/ppermute | solution.py:234
  94.6 12.0 %collective-permute-start.3 = (bf16[512,128]{1,0:T(8,128)(2,1)S(1)}, bf16[512,128]{1,0:T(8,128)(2,1)S(1)}, u32[]{:S(2)}, u32[]{:S(2)}) collective-permute-start(bf16[512,128]{1,0:T(8,128)(2,1)S(1)} %get-tuple-element.25), channel_id=1, source_target_pairs={{0,2},{1,3},{2,0},{3,1},{4,6},{5,7},{6,4},{7,5},{8,10},{9,11},{10,... | collective-permute-start | bytes 393224 | tf_op jit(solution)/shard_map/ppermute | solution.py:234
  96.3 10.4 %collective-permute-start.4 = (bf16[512,128]{1,0:T(8,128)(2,1)S(1)}, bf16[512,128]{1,0:T(8,128)(2,1)S(1)}, u32[]{:S(2)}, u32[]{:S(2)}) collective-permute-start(bf16[512,128]{1,0:T(8,128)(2,1)S(1)} %get-tuple-element.26), channel_id=1, source_target_pairs={{0,3},{1,2},{2,1},{3,0},{4,7},{5,6},{6,5},{7,4},{8,11},{9,10},{10,... | collective-permute-start | bytes 393224 | tf_op jit(solution)/shard_map/ppermute | solution.py:234
  97.1 5.8 %collective-permute-start.12 = (f32[32,256]{1,0:T(8,128)S(1)}, f32[32,256]{1,0:T(8,128)S(1)}, u32[]{:S(2)}, u32[]{:S(2)}) collective-permute-start(f32[32,256]{1,0:T(8,128)S(1)} %add_add_fusion), channel_id=1, source_target_pairs={{0,32},{4,36},{8,40},{12,44},{16,48},{20,52},{24,56},{28,60},{32,0... | collective-permute-start | bytes 98312 | tf_op jit(solution)/shard_map/ppermute | solution.py:234
  102.8 5.7 %collective-permute-start.13 = (f32[32,256]{1,0:T(8,128)S(1)}, f32[32,256]{1,0:T(8,128)S(1)}, u32[]{:S(2)}, u32[]{:S(2)}) collective-permute-start(f32[32,256]{1,0:T(8,128)S(1)} %add.61), channel_id=1, source_target_pairs={{0,64},{4,68},{8,72},{12,76},{16,80},{20,84},{24,88},{28,92},{32,9... | collective-permute-start | bytes 98312 | tf_op jit(solution)/shard_map/ppermute | solution.py:234
  110.0 7.3 %collective-permute-start.14 = (f32[32,256]{1,0:T(8,128)S(1)}, f32[32,256]{1,0:T(8,128)S(1)}, u32[]{:S(2)}, u32[]{:S(2)}) collective-permute-start(f32[32,256]{1,0:T(8,128)S(1)} %add.62), channel_id=1, source_target_pairs={{0,128},{4,132},{8,136},{12,140},{16,144},{20,148},{24,152},{28,15... | collective-permute-start | bytes 98312 | tf_op jit(solution)/shard_map/ppermute | solution.py:234
  117.4 5.9 %collective-permute-start.17 = (f32[32,256]{1,0:T(8,128)S(1)}, f32[32,256]{1,0:T(8,128)S(1)}, u32[]{:S(2)}, u32[]{:S(2)}) collective-permute-start(f32[32,256]{1,0:T(8,128)S(1)} %add.63), channel_id=1, source_target_pairs={{0,8},{4,12},{8,0},{12,4},{16,24},{20,28},{24,16},{28,20},{32,40},... | collective-permute-start | bytes 98312 | tf_op jit(solution)/shard_map/ppermute | solution.py:234
  117.8 16.3 %collective-permute-start.19 = (bf16[512,256]{1,0:T(8,128)(2,1)S(1)}, bf16[512,256]{1,0:T(8,128)(2,1)S(1)}, u32[]{:S(2)}, u32[]{:S(2)}) collective-permute-start(bf16[512,256]{1,0:T(8,128)(2,1)S(1)} %shard_map.107.refs_0_), channel_id=1, source_target_pairs={{0,1},{1,2},{2,3},{3,0},{4,5},{5,6},{6,7},{7,4},{8,9},{9,10},{10,1... | collective-permute-start | bytes 786440 | tf_op jit(solution)/shard_map/ppermute | solution.py:226
  118.1 16.0 %collective-permute-start.20 = (bf16[512,256]{1,0:T(8,128)(2,1)S(1)}, bf16[512,256]{1,0:T(8,128)(2,1)S(1)}, u32[]{:S(2)}, u32[]{:S(2)}) collective-permute-start(bf16[512,256]{1,0:T(8,128)(2,1)S(1)} %shard_map.107.refs_0_), channel_id=1, source_target_pairs={{0,2},{1,3},{2,0},{3,1},{4,6},{5,7},{6,4},{7,5},{8,10},{9,11},{10,... | collective-permute-start | bytes 786440 | tf_op jit(solution)/shard_map/ppermute | solution.py:226
  120.3 13.7 %collective-permute-start.21 = (bf16[512,256]{1,0:T(8,128)(2,1)S(1)}, bf16[512,256]{1,0:T(8,128)(2,1)S(1)}, u32[]{:S(2)}, u32[]{:S(2)}) collective-permute-start(bf16[512,256]{1,0:T(8,128)(2,1)S(1)} %shard_map.107.refs_0_), channel_id=1, source_target_pairs={{0,3},{1,0},{2,1},{3,2},{4,7},{5,4},{6,5},{7,6},{8,11},{9,8},{10,9... | collective-permute-start | bytes 786440 | tf_op jit(solution)/shard_map/ppermute | solution.py:226
  121.5 4.3 %collective-permute-start.15 = (f32[32,256]{1,0:T(8,128)S(1)}, f32[32,256]{1,0:T(8,128)S(1)}, u32[]{:S(2)}, u32[]{:S(2)}) collective-permute-start(f32[32,256]{1,0:T(8,128)S(1)} %add.63), channel_id=1, source_target_pairs={{0,24},{4,28},{8,16},{12,20},{16,8},{20,12},{24,0},{28,4},{32,56},... | collective-permute-start | bytes 98312 | tf_op jit(solution)/shard_map/ppermute | solution.py:234
  123.3 4.3 %collective-permute-start.16 = (f32[32,256]{1,0:T(8,128)S(1)}, f32[32,256]{1,0:T(8,128)S(1)}, u32[]{:S(2)}, u32[]{:S(2)}) collective-permute-start(f32[32,256]{1,0:T(8,128)S(1)} %add.63), channel_id=1, source_target_pairs={{0,16},{4,20},{8,24},{12,28},{16,0},{20,4},{24,8},{28,12},{32,48},... | collective-permute-start | bytes 98312 | tf_op jit(solution)/shard_map/ppermute | solution.py:234
  127.6 5.8 %collective-permute-start.18 = (f32[128,256]{1,0:T(8,128)S(1)}, f32[128,256]{1,0:T(8,128)S(1)}, u32[]{:S(2)}, u32[]{:S(2)}) collective-permute-start(f32[128,256]{1,0:T(8,128)S(1)} %maximum_select_fusion.1), channel_id=1, source_target_pairs={{0,4},{4,0},{8,12},{12,8},{16,20},{20,16},{24,28},{28,24},{32,36},... | collective-permute-start | bytes 393224 | tf_op jit(solution)/shard_map/ppermute | solution.py:234
